TPU v7x, 512 devices: a whole 4x8x8 slice. The times are simulated.
512 devices in a mesh: dp: 32 (over x, z), tensor: 16 (over y, core).
Axes of the slice: x: 4, y: 8, z: 8, core: 2. Of those that a mesh axis runs over, the one named last changes fastest.
Arguments:
- inputs: bfloat16 [16384, 5120], P('dp', 'tensor'), may hold values from -6 to 6
- out_grads: bfloat16 [2, 16384, 12800], P(None, 'dp', 'tensor'), may hold values from -0.046875 to 0.046875
- projector: bfloat16 [5120, 128], replicated, may hold values from -0.078125 to 0.078125
- first_moment: float32 [2, 128, 12800], P(None, 'dp', 'tensor'), may hold values from -4 to 4
- second_moment: float32 [2, 128, 12800], P(None, 'dp', 'tensor'), may hold values from 0.0001 to 0.01
Outputs:
- updates: bfloat16 [2, 5120, 12800], P(None, 'dp', 'tensor')
- new_first: float32 [2, 128, 12800], P(None, 'dp', 'tensor')
- new_second: float32 [2, 128, 12800], P(None, 'dp', 'tensor')
All inputs are finite; a program needn't handle non-finite values.
Results may differ from a plain program's by a relative error of at most 0.0055.
Values may be sent and summed in bfloat16 or wider, within the bound.
No kernel may reach another device: no remote copies, remote signals or barrier semaphores. Data moves between devices by JAX's collectives and lax.ppermute only.
A program may use at most 64 MiB of HBM per device.

v0:
```python
import jax
import jax.numpy as jnp
from jax import lax
from jax.sharding import PartitionSpec as P


def per_device(inputs, out_grads, projector, first_moment, second_moment):
    feat_rows = inputs.shape[1]
    start_row = lax.axis_index("tensor") * feat_rows
    own_rows = lax.dynamic_slice_in_dim(projector, start_row, feat_rows, 0)
    partial_sum = jnp.dot(inputs, own_rows, preferred_element_type=jnp.float32)
    summed = lax.psum(partial_sum, "tensor")
    low = summed.astype(jnp.bfloat16)
    projected = jnp.einsum("tr,ktc->krc", low, out_grads, preferred_element_type=jnp.float32)
    owned = lax.psum_scatter(projected, "dp", scatter_dimension=1, tiled=True)
    new_first = 0.9 * first_moment + 0.1 * owned
    new_second = 0.999 * second_moment + 0.001 * owned * owned
    first_fix = 1.0 - 0.9**10
    second_fix = 1.0 - 0.999**10
    direction = (new_first / first_fix / (jnp.sqrt(new_second / second_fix) + 1e-08)).astype(
        jnp.bfloat16
    )
    out_rows = projector.shape[0] // lax.axis_size("dp")
    block_rows = lax.dynamic_slice_in_dim(projector, lax.axis_index("dp") * out_rows, out_rows, 0)
    expanded = jnp.einsum(
        "dr,krc->kdc",
        block_rows,
        lax.all_gather(direction, "dp", axis=1, tiled=True),
        preferred_element_type=jnp.float32,
    )
    return (expanded.astype(jnp.bfloat16), new_first, new_second)


def solution(mesh):
    return jax.shard_map(
        per_device,
        mesh=mesh,
        in_specs=(
            P("dp", "tensor"),
            P(None, "dp", "tensor"),
            P(),
            P(None, "dp", "tensor"),
            P(None, "dp", "tensor"),
        ),
        out_specs=(P(None, "dp", "tensor"), P(None, "dp", "tensor"), P(None, "dp", "tensor")),
        check_vma=False,
    )
```

profile of v0, /device:TPU:6, one launch (start us, length us, event | category | flops | bytes accessed | tf_op | source)
XLA Modules:
  0.0 281.9 jit_solution(13868928316216459604)
XLA Ops:
  7.2 0.0 copy-start
  7.2 0.0 all-reduce.4.cloned.1.call-start
  7.2 1.5 convolution_bitcast_fusion.1
  8.7 50.8 %all-reduce.5 = bf16[512,128]{1,0:T(8,128)(2,1)S(1)} all-reduce(f32[512,128]{1,0:T(8,128)S(1)} %convolution_bitcast_fusion.1), channel_id=1, replica_groups=mesh['dp'=32,'tensor'=16] {'tensor'}, use_global_device_ids=true, to_apply=%region_0.0 | all-reduce | flops 65536 | bytes 393216 | tf_op jit(solution)/shard_map/psum | solution.py:12
  59.5 0.0 copy-done
  59.5 0.6 convolution_bitcast_fusion
  60.1 0.0 copy-start.1
  60.1 0.0 copy-start.2
  60.2 1.3 copy.16
  61.5 0.0 all-reduce.4.cloned.1.call-update
  61.5 1.3 dynamic-slice
  63.4 159.3 %all-reduce.4.cloned.1.call-done = f32[2,128,800]{2,0,1:T(2,128)} async-done(((f32[2,128,800]{2,0,1:T(2,128)}), f32[2,128,800]{2,0,1:T(2,128)}) %all-reduce.4.cloned.1.call-update) | async-done | bytes 819216
  222.8 0.0 copy-done.1
  222.8 0.0 copy-done.2
  222.8 0.8 fusion.9
  223.6 48.3 %all_gather.3 = bf16[2,128,800]{2,0,1:T(2,128)(2,1)S(1)} all-gather(bf16[2,4,800]{2,0,1:T(2,128)(2,1)S(1)} %get-tuple-element.9), channel_id=1, replica_groups=mesh['dp'=32,'tensor'=16] {'dp'}, dimensions={1}, use_global_device_ids=true | all-gather | bytes 422400 | tf_op jit(solution)/shard_map/all_gather | solution.py:28
  271.9 0.6 copy.19
  272.5 0.6 copy.20
  273.2 1.9 fusion
Async XLA Ops:
  7.2 52.4 %copy-start = (bf16[2,512,800]{1,2,0:T(8,128)(2,1)S(1)}, bf16[2,512,800]{1,2,0:T(8,128)(2,1)}, u32[]{:S(2)}) copy-start(bf16[2,512,800]{1,2,0:T(8,128)(2,1)} %param.6) | copy-start | bytes 4915204
  7.2 215.6 %all-reduce.4.cloned.1.call-start = ((), (), s32[]{:S(2)}) async-start(), calls=%async_computation | async-start | bytes 1835008
  60.1 162.6 %copy-start.1 = (f32[2,4,800]{2,1,0:T(4,128)S(1)}, f32[2,4,800]{2,1,0:T(4,128)}, u32[]{:S(2)}) copy-start(f32[2,4,800]{2,1,0:T(4,128)} %param.8) | copy-start | bytes 76804
  60.1 162.6 %copy-start.2 = (f32[2,4,800]{2,1,0:T(4,128)S(1)}, f32[2,4,800]{2,1,0:T(4,128)}, u32[]{:S(2)}) copy-start(f32[2,4,800]{2,1,0:T(4,128)} %param.9) | copy-start | bytes 76804
Sparse Core Ops, SparseCore 0:
  61.6 161.0 all-reduce.3
where the time goes:
time: 284 us; the launch traced here: 282 us
  waiting for transfers between devices  159 us (56%)
  blocking collectives  99.1 us (35%)
  between operations  14.7 us (5%)
  matrix products  3.94 us (1%)
  local copies, waits for them, and re-layouts  3.85 us (1%)
    unnamed x2, waiting for transfers between devices  159 us
    psum x1, blocking collectives, per_device(): summed = lax.psum(partial_sum, 'tensor')  50.8 us
    all_gather x1, blocking collectives, per_device(): lax.all_gather(direction, 'dp', axis=1, tiled=True)  48.3 us
  transfers between devices with their start and end apart: 1, of which 1 were waited for; matrix products, arithmetic and copies ran while one was open for 0% of the time, Pallas kernels for 0%

commit v1 on v0

v1 whole, which is shorter than its diff:
```python
import jax
import jax.numpy as jnp
from jax import lax
from jax.sharding import PartitionSpec as P


def exchange(blocks, axis):
    return lax.all_to_all(blocks, axis, 0, 0)


def gather(block, axis):
    return exchange(jnp.broadcast_to(block[None], (lax.axis_size(axis), *block.shape)), axis)


def per_device(inputs, out_grads, projector, first_moment, second_moment):
    tokens, feat_rows = inputs.shape
    n_grads, _, columns = out_grads.shape
    rank = projector.shape[1]
    n_dp, n_tensor = lax.axis_size("dp"), lax.axis_size("tensor")
    own_rows = lax.dynamic_slice_in_dim(
        projector, lax.axis_index("tensor") * feat_rows, feat_rows, 0
    )
    partial_sum = jnp.dot(inputs, own_rows, preferred_element_type=jnp.float32)
    parts = exchange(
        partial_sum.astype(jnp.bfloat16).reshape(n_tensor, tokens // n_tensor, rank), "tensor"
    )
    own_low = jnp.sum(parts.astype(jnp.float32), axis=0).astype(jnp.bfloat16)
    low = gather(own_low, "tensor").reshape(tokens, rank)
    projected = jnp.einsum("tr,ktc->krc", low, out_grads, preferred_element_type=jnp.float32)
    own_rank = rank // n_dp
    sent = projected.astype(jnp.bfloat16).reshape(n_grads, n_dp, own_rank, columns)
    sent = sent.transpose(1, 0, 2, 3).reshape(n_dp, n_grads * own_rank, columns)
    owned = jnp.sum(exchange(sent, "dp").astype(jnp.float32), axis=0)
    owned = owned.reshape(n_grads, own_rank, columns)
    new_first = 0.9 * first_moment + 0.1 * owned
    new_second = 0.999 * second_moment + 0.001 * owned * owned
    first_fix = 1.0 - 0.9**10
    second_fix = 1.0 - 0.999**10
    direction = (new_first / first_fix / (jnp.sqrt(new_second / second_fix) + 1e-08)).astype(
        jnp.bfloat16
    )
    every = gather(direction.reshape(n_grads * own_rank, columns), "dp")
    every = every.reshape(n_dp, n_grads, own_rank, columns).transpose(1, 0, 2, 3)
    every = every.reshape(n_grads, rank, columns)
    out_rows = projector.shape[0] // n_dp
    block_rows = lax.dynamic_slice_in_dim(projector, lax.axis_index("dp") * out_rows, out_rows, 0)
    expanded = jnp.einsum("dr,krc->kdc", block_rows, every, preferred_element_type=jnp.float32)
    return (expanded.astype(jnp.bfloat16), new_first, new_second)


def solution(mesh):
    return jax.shard_map(
        per_device,
        mesh=mesh,
        in_specs=(
            P("dp", "tensor"),
            P(None, "dp", "tensor"),
            P(),
            P(None, "dp", "tensor"),
            P(None, "dp", "tensor"),
        ),
        out_specs=(P(None, "dp", "tensor"), P(None, "dp", "tensor"), P(None, "dp", "tensor")),
        check_vma=False,
    )
```

time: 284 us -> 85.9 us (0.30)
  the two profiles are of different devices: /device:TPU:6 before, /device:TPU:64 now
where the time goes in v1:
time: 85.9 us; the launch traced here: 85.5 us
  blocking collectives  56.8 us (66%)
  waiting for transfers between devices  16 us (19%)
  starting transfers between devices  4.93 us (6%)
  matrix products  3.86 us (4%)
  local copies, waits for them, and re-layouts  2.38 us (3%)
    all_to_all x3, blocking collectives, exchange(): return lax.all_to_all(blocks, axis, 0, 0)  56.8 us
    all_to_all x1, waiting for transfers between devices, exchange(): return lax.all_to_all(blocks, axis, 0, 0)  16 us
    all_to_all x1, starting transfers between devices, exchange(): return lax.all_to_all(blocks, axis, 0, 0)  4.93 us
    dot_general x1, matrix products, per_device(): jnp.einsum('dr,krc->kdc', block_rows, every, preferred_element_type=jnp.f...  1.9 us
  transfers between devices with their start and end apart: 1, of which 1 were waited for; matrix products, arithmetic and copies ran while one was open for 0% of the time, Pallas kernels for 0%

profile of v1, /device:TPU:64, one launch (start us, length us, event | category | flops | bytes accessed | tf_op | source)
XLA Modules:
  0.0 85.5 jit_solution(5476493656142133035)
XLA Ops:
  0.6 0.0 copy-start
  0.7 1.4 %fusion.2 = bf16[512,128]{0,1:T(8,128)(2,1)S(1)} fusion(bf16[512,320]{0,1:T(8,128)(2,1)} %param.5, bf16[5120,128]{1,0:T(8,128)(2,1)} %param.7, s32[]{:T(128)S(6)} %select_n.6), kind=kOutput, calls=%fused_computation.5 | convolution fusion | flops 42008576 | bytes 540676 | tf_op jit(solution)/shard_map/dot_general | solution.py:23
  2.0 0.1 copy.13
  2.2 15.7 %all_to_all.20 = bf16[16,32,128]{2,1,0:T(8,128)(2,1)S(1)} all-to-all(bf16[16,32,128]{2,1,0:T(8,128)(2,1)S(1)} %bitcast.29), channel_id=1, replica_groups=mesh['dp'=32,'tensor'=16] {'tensor'}, dimensions={0} | all-to-all | bytes 262144 | tf_op jit(solution)/shard_map/all_to_all | solution.py:8
  18.0 11.6 %all_to_all.21 = bf16[16,32,128]{2,1,0:T(8,128)(2,1)S(1)} all-to-all(bf16[16,32,128]{2,1,0:T(8,128)(2,1)S(1)} %broadcast_in_dim.6), channel_id=1, replica_groups=mesh['dp'=32,'tensor'=16] {'tensor'}, dimensions={0} | all-to-all | bytes 262144 | tf_op jit(solution)/shard_map/all_to_all | solution.py:8
  29.6 0.0 copy-done
  29.6 0.6 fusion.1
  30.1 0.7 copy.14
  30.8 0.1 copy.15
  30.9 0.0 copy-start.1
  30.9 0.0 copy-start.2
  30.9 0.1 copy.16
  31.1 29.5 %all_to_all.22 = bf16[32,8,800]{2,1,0:T(8,128)(2,1)S(1)} all-to-all(bf16[32,8,800]{2,1,0:T(8,128)(2,1)S(1)} %copy.16), channel_id=1, replica_groups=mesh['dp'=32,'tensor'=16] {'dp'}, dimensions={0} | all-to-all | bytes 819200 | tf_op jit(solution)/shard_map/all_to_all | solution.py:8
  60.6 0.1 convert_reduce_fusion
  60.7 0.0 copy-done.1
  60.7 0.0 copy-done.2
  60.7 0.7 fusion.8
  61.4 0.8 broadcast_in_dim.15
  62.2 4.9 %all-to-all-start.3 = ((bf16[32,8,800]{2,1,0:T(8,128)(2,1)}), bf16[32,8,800]{2,1,0:T(8,128)(2,1)S(1)}, u32[]{:S(2)}, u32[]{:S(2)}) async-start(bf16[32,8,800]{2,1,0:T(8,128)(2,1)} %broadcast_in_dim.15), calls=%async_computation.3 | async-start | bytes 917504 | tf_op jit(solution)/shard_map/all_to_all | solution.py:8
  67.1 16.0 %all-to-all-done.3 = bf16[32,8,800]{2,1,0:T(8,128)(2,1)S(1)} async-done(((bf16[32,8,800]{2,1,0:T(8,128)(2,1)}), bf16[32,8,800]{2,1,0:T(8,128)(2,1)S(1)}, u32[]{:S(2)}, u32[]{:S(2)}) %all-to-all-start.3) | async-done | bytes 409632 | tf_op jit(solution)/shard_map/all_to_all | solution.py:8
  83.1 0.5 copy.18
  83.6 1.9 %fusion = bf16[2,160,800]{2,1,0:T(8,128)(2,1)} fusion(bf16[2,128,800]{2,0,1:T(2,128)(2,1)S(1)} %bitcast.26, bf16[5120,128]{1,0:T(8,128)(2,1)} %param.7, s32[]{:T(128)S(6)} %select_n.7), kind=kOutput, calls=%fused_computation.2 | convolution fusion | flops 65792000 | bytes 962564 | tf_op jit(solution)/shard_map/dr,krc->kdc/dot_general | solution.py:47
  (5 shorter events, 0.1 us)
Async XLA Ops:
  0.6 28.9 %copy-start = (bf16[2,512,800]{1,2,0:T(8,128)(2,1)S(1)}, bf16[2,512,800]{1,2,0:T(8,128)(2,1)}, u32[]{:S(2)}) copy-start(bf16[2,512,800]{1,2,0:T(8,128)(2,1)} %param.6) | copy-start | bytes 4915204
  30.9 29.8 %copy-start.1 = (f32[2,4,800]{2,1,0:T(4,128)S(1)}, f32[2,4,800]{2,1,0:T(4,128)}, u32[]{:S(2)}) copy-start(f32[2,4,800]{2,1,0:T(4,128)} %param.8) | copy-start | bytes 76804
  30.9 29.8 %copy-start.2 = (f32[2,4,800]{2,1,0:T(4,128)S(1)}, f32[2,4,800]{2,1,0:T(4,128)}, u32[]{:S(2)}) copy-start(f32[2,4,800]{2,1,0:T(4,128)} %param.9) | copy-start | bytes 76804
  62.2 20.9 %all-to-all-start.3 = ((bf16[32,8,800]{2,1,0:T(8,128)(2,1)}), bf16[32,8,800]{2,1,0:T(8,128)(2,1)S(1)}, u32[]{:S(2)}, u32[]{:S(2)}) async-start(bf16[32,8,800]{2,1,0:T(8,128)(2,1)} %broadcast_in_dim.15), calls=%async_computation.3 | async-start | bytes 917504 | tf_op jit(solution)/shard_map/all_to_all | solution.py:8

commit v2 on v0

v2 whole, which is shorter than its diff:
```python
import jax
import jax.numpy as jnp
from jax import lax
from jax.experimental import pallas as pl
from jax.experimental.pallas import tpu as pltpu
from jax.sharding import PartitionSpec as P

FIRST_FIX = 1.0 - 0.9**10
SECOND_FIX = 1.0 - 0.999**10
PARAMS = pltpu.CompilerParams(vmem_limit_bytes=16 * 1024 * 1024)
VMEM = pl.BlockSpec(memory_space=pltpu.VMEM)
HBM = pl.BlockSpec(memory_space=pltpu.HBM)


def exchange(blocks, axis):
    return lax.all_to_all(blocks, axis, 0, 0)


def cost(flops, nbytes):
    return pl.CostEstimate(flops=flops, bytes_accessed=nbytes, transcendentals=0)


def low_kernel(x_ref, p_ref, parts_ref, rows_ref, x_buf, p_buf, sems):
    n, height, tokens = parts_ref.shape
    feats, out_rows = x_ref.shape[0], rows_ref.shape[0]
    own = pl.multiple_of(lax.axis_index("tensor") * feats, 16)
    block = pl.multiple_of(lax.axis_index("dp") * out_rows, 16)
    copies = (
        pltpu.make_async_copy(p_ref.at[pl.ds(own, feats)], p_buf, sems.at[0]),
        pltpu.make_async_copy(x_ref, x_buf, sems.at[1]),
        pltpu.make_async_copy(p_ref.at[pl.ds(block, out_rows)], rows_ref, sems.at[2]),
    )
    for copy in copies:
        copy.start()
    copies[0].wait()
    copies[1].wait()
    partial_sum = lax.dot_general(
        p_buf[...], x_buf[...], (((0,), (0,)), ((), ())), preferred_element_type=jnp.float32
    )
    parts_ref[...] = partial_sum.astype(parts_ref.dtype).reshape(n, height, tokens)
    copies[2].wait()


def low_parts(inputs, projector, n_tensor, n_dp):
    tokens, feats = inputs.shape
    width, rank = projector.shape
    bf16 = jnp.bfloat16
    return pl.pallas_call(
        low_kernel,
        out_shape=(
            pltpu.VMEM((n_tensor, rank // n_tensor, tokens), bf16),
            pltpu.VMEM((width // n_dp, rank), bf16),
        ),
        in_specs=[HBM, HBM],
        out_specs=[VMEM, VMEM],
        scratch_shapes=[
            pltpu.VMEM((feats, tokens), bf16),
            pltpu.VMEM((feats, rank), bf16),
            pltpu.SemaphoreType.DMA((3,)),
        ],
        compiler_params=PARAMS,
        cost_estimate=cost(2 * tokens * feats * rank, 2 * feats * (tokens + rank)),
    )(inputs.T, projector)


def halves(shape):
    return lax.broadcasted_iota(jnp.int32, shape, 1) < shape[1] // 2


def project_kernel(low_ref, grads_ref, out_ref):
    groups, height, tokens = low_ref.shape
    columns = grads_ref.shape[1]
    low = low_ref[...].reshape(groups * height, tokens)
    gate, up = (
        lax.dot_general(
            low, grads_ref[k], (((1,), (1,)), ((), ())), preferred_element_type=jnp.float32
        ).reshape(groups, height, columns)
        for k in range(2)
    )
    upper = halves(gate.shape)
    turn = height // 2
    out_ref[:, 0] = jnp.where(upper, gate, pltpu.roll(up, turn, 1)).astype(out_ref.dtype)
    out_ref[:, 1] = jnp.where(upper, pltpu.roll(gate, turn, 1), up).astype(out_ref.dtype)


def project(low, grads):
    groups, height, tokens = low.shape
    columns = grads.shape[1]
    return pl.pallas_call(
        project_kernel,
        out_shape=pltpu.VMEM((groups, 2, height, columns), jnp.bfloat16),
        in_specs=[VMEM, VMEM],
        out_specs=VMEM,
        compiler_params=PARAMS,
        cost_estimate=cost(4 * groups * height * tokens * columns, 4 * tokens * columns),
    )(low, grads)


def adam_kernel(parts_ref, first_ref, second_ref, out_ref, new_first_ref, new_second_ref):
    own = jnp.sum(parts_ref[...].astype(jnp.float32), axis=0)
    n_grads, height, _ = first_ref.shape
    direction = []
    for k in range(n_grads):
        projected = own[k * height : (k + 1) * height]
        first = 0.9 * first_ref[k] + 0.1 * projected
        second = 0.999 * second_ref[k] + 0.001 * projected * projected
        new_first_ref[k] = first
        new_second_ref[k] = second
        direction.append(first / FIRST_FIX / (jnp.sqrt(second / SECOND_FIX) + 1e-08))
    direction = jnp.concatenate(direction, axis=0).astype(out_ref.dtype)
    out_ref[...] = jnp.broadcast_to(direction[None], out_ref.shape)


def adam(parts, first, second):
    return pl.pallas_call(
        adam_kernel,
        out_shape=(
            pltpu.VMEM(parts.shape, jnp.bfloat16),
            pltpu.VMEM(first.shape, jnp.float32),
            pltpu.VMEM(second.shape, jnp.float32),
        ),
        in_specs=[VMEM] * 3,
        out_specs=[VMEM] * 3,
        compiler_params=PARAMS,
        cost_estimate=cost(parts.size, 4 * parts.size),
    )(parts, first, second)


def expand_kernel(
    rows_ref, dirs_ref, first_ref, second_ref, out_ref, new_first_ref, new_second_ref, buf, sems
):
    pairs, _, height, columns = dirs_ref.shape
    copies = [
        pltpu.make_async_copy(first_ref, new_first_ref, sems.at[2]),
        pltpu.make_async_copy(second_ref, new_second_ref, sems.at[3]),
    ]
    for copy in copies:
        copy.start()
    even = dirs_ref[:, 0].astype(jnp.float32)
    odd = dirs_ref[:, 1].astype(jnp.float32)
    upper = halves(even.shape)
    turn = height // 2
    ordered = (
        jnp.where(upper, even, pltpu.roll(odd, turn, 1)),
        jnp.where(upper, pltpu.roll(even, turn, 1), odd),
    )
    for k in range(2):
        direction = ordered[k].astype(jnp.bfloat16).reshape(pairs * height, columns)
        update = jnp.dot(rows_ref[...], direction, preferred_element_type=jnp.float32)
        buf[k] = update.astype(buf.dtype)
        copies.append(pltpu.make_async_copy(buf.at[k], out_ref.at[k], sems.at[k]))
        copies[-1].start()
    for copy in copies:
        copy.wait()


def expand(rows, dirs, first, second):
    out_rows, rank = rows.shape
    columns = dirs.shape[-1]
    shape = (2, out_rows, columns)
    return pl.pallas_call(
        expand_kernel,
        out_shape=(
            pltpu.HBM(shape, jnp.bfloat16),
            pltpu.HBM(first.shape, first.dtype),
            pltpu.HBM(second.shape, second.dtype),
        ),
        in_specs=[VMEM] * 4,
        out_specs=[HBM] * 3,
        scratch_shapes=[pltpu.VMEM(shape, jnp.bfloat16), pltpu.SemaphoreType.DMA((4,))],
        compiler_params=PARAMS,
        cost_estimate=cost(4 * out_rows * rank * columns, 4 * out_rows * columns),
    )(rows, dirs, first, second)


def per_device(inputs, out_grads, projector, first_moment, second_moment):
    n_dp, n_tensor = lax.axis_size("dp"), lax.axis_size("tensor")
    columns = out_grads.shape[2]
    parts, rows = low_parts(inputs, projector, n_tensor, n_dp)
    parts = exchange(parts, "tensor")
    own_low = jnp.sum(parts.astype(jnp.float32), axis=0).astype(jnp.bfloat16)
    low = exchange(jnp.broadcast_to(own_low[None], parts.shape), "tensor")
    sent = project(low, out_grads.transpose(0, 2, 1))
    received = exchange(sent.reshape(n_dp, -1, columns), "dp")
    direction, new_first, new_second = adam(received, first_moment, second_moment)
    every = exchange(direction, "dp").reshape(sent.shape)
    return expand(rows, every, new_first, new_second)


def solution(mesh):
    return jax.shard_map(
        per_device,
        mesh=mesh,
        in_specs=(
            P("dp", "tensor"),
            P(None, "dp", "tensor"),
            P(),
            P(None, "dp", "tensor"),
            P(None, "dp", "tensor"),
        ),
        out_specs=(P(None, "dp", "tensor"), P(None, "dp", "tensor"), P(None, "dp", "tensor")),
        check_vma=False,
    )
```

time: 284 us -> 83.4 us (0.29)
  the two profiles are of different devices: /device:TPU:6 before, /device:TPU:64 now
where the time goes in v2:
time: 83.4 us; the launch traced here: 83.1 us
  blocking collectives  77.6 us (93%)
  Pallas kernels  2.44 us (3%)
  local copies, waits for them, and re-layouts  2.43 us (3%)
    all_to_all x4, blocking collectives, exchange(): return lax.all_to_all(blocks, axis, 0, 0)  77.6 us
    unnamed x10, local copies, waits for them, and re-layouts  2.41 us

profile of v2, /device:TPU:64, one launch (start us, length us, event | category | flops | bytes accessed | tf_op | source)
XLA Modules:
  0.0 83.1 jit_solution(503072380020029666)
XLA Ops:
  0.6 0.0 copy-start
  0.6 0.0 copy-start.1
  0.7 1.4 %copy-done.1 = bf16[5120,128]{1,0:T(8,128)(2,1)S(1)} copy-done((bf16[5120,128]{1,0:T(8,128)(2,1)S(1)}, bf16[5120,128]{1,0:T(8,128)(2,1)}, u32[]{:S(2)}) %copy-start.1) | copy-done | bytes 1310744
  2.1 0.0 copy-start.2
  2.1 1.0 %copy-done.2 = bf16[512,320]{0,1:T(8,128)(2,1)S(1)} copy-done((bf16[512,320]{0,1:T(8,128)(2,1)S(1)}, bf16[512,320]{0,1:T(8,128)(2,1)}, u32[]{:S(2)}) %copy-start.2) | copy-done | bytes 327704
  3.1 0.5 shard_map.76
  3.6 15.8 %all_to_all.20 = bf16[16,8,512]{2,1,0:T(8,128)(2,1)S(1)} all-to-all(bf16[16,8,512]{2,1,0:T(8,128)(2,1)S(1)} %get-tuple-element.9), channel_id=1, replica_groups=mesh['dp'=32,'tensor'=16] {'tensor'}, dimensions={0} | all-to-all | bytes 262144 | tf_op jit(solution)/shard_map/all_to_all | solution.py:16
  19.4 11.6 %all_to_all.21.low_ref = bf16[16,8,512]{2,1,0:T(8,128)(2,1)S(1)} all-to-all(bf16[16,8,512]{2,1,0:T(8,128)(2,1)S(1)} %broadcast_in_dim.2), channel_id=1, replica_groups=mesh['dp'=32,'tensor'=16] {'tensor'}, dimensions={0} | all-to-all | bytes 262144 | tf_op jit(solution)/shard_map/all_to_all | solution.py:16
  31.0 0.0 copy-start.3
  31.0 0.0 copy-start.4
  31.0 0.0 copy-done
  31.0 0.7 shard_map.77
  31.7 29.5 %all_to_all.22.parts_ref = bf16[32,8,800]{2,1,0:T(8,128)(2,1)S(1)} all-to-all(bf16[32,8,800]{2,1,0:T(8,128)(2,1)S(1)} %bitcast.5), channel_id=1, replica_groups=mesh['dp'=32,'tensor'=16] {'dp'}, dimensions={0} | all-to-all | bytes 819200 | tf_op jit(solution)/shard_map/all_to_all | solution.py:16
  61.2 0.0 copy-done.3
  61.2 0.0 copy-done.4
  61.2 0.1 shard_map.78
  61.3 20.7 %all_to_all.23 = bf16[32,8,800]{2,1,0:T(8,128)(2,1)S(1)} all-to-all(bf16[32,8,800]{2,1,0:T(8,128)(2,1)S(1)} %get-tuple-element.10), channel_id=1, replica_groups=mesh['dp'=32,'tensor'=16] {'dp'}, dimensions={0} | all-to-all | bytes 819200 | tf_op jit(solution)/shard_map/all_to_all | solution.py:16
  82.0 1.1 %shard_map.79 = (bf16[2,160,800]{2,1,0:T(8,128)(2,1)}, f32[2,4,800]{2,1,0:T(4,128)}, f32[2,4,800]{2,1,0:T(4,128)}) custom-call(bf16[160,128]{1,0:T(8,128)(2,1)S(1)} %get-tuple-element.8.rows_ref, bf16[16,2,8,800]{3,2,1,0:T(8,128)(2,1)S(1)} %bitcast.4, f32[2,4,800]{2,1,0:T(4,128)S(1)} %get-tuple-element.11.first_ref, ...), custom_call_target="tpu_custom_call" | custom-call | flops 65536000 | bytes 512000 | tf_op jit(solution)/shard_map/pallas_call | solution.py:161
  (2 shorter events, 0.0 us)
Async XLA Ops:
  0.6 30.3 %copy-start = (bf16[2,512,800]{1,2,0:T(8,128)(2,1)S(1)}, bf16[2,512,800]{1,2,0:T(8,128)(2,1)}, u32[]{:S(2)}) copy-start(bf16[2,512,800]{1,2,0:T(8,128)(2,1)} %param.6) | copy-start | bytes 4915204
  0.6 1.4 %copy-start.1 = (bf16[5120,128]{1,0:T(8,128)(2,1)S(1)}, bf16[5120,128]{1,0:T(8,128)(2,1)}, u32[]{:S(2)}) copy-start(bf16[5120,128]{1,0:T(8,128)(2,1)} %p_ref.1) | copy-start | bytes 3932164
  2.1 1.0 %copy-start.2 = (bf16[512,320]{0,1:T(8,128)(2,1)S(1)}, bf16[512,320]{0,1:T(8,128)(2,1)}, u32[]{:S(2)}) copy-start(bf16[512,320]{0,1:T(8,128)(2,1)} %param.5) | copy-start | bytes 983044
  31.0 30.2 %copy-start.3 = (f32[2,4,800]{2,1,0:T(4,128)S(1)}, f32[2,4,800]{2,1,0:T(4,128)}, u32[]{:S(2)}) copy-start(f32[2,4,800]{2,1,0:T(4,128)} %first_ref.1) | copy-start | bytes 76804
  31.0 30.2 %copy-start.4 = (f32[2,4,800]{2,1,0:T(4,128)S(1)}, f32[2,4,800]{2,1,0:T(4,128)}, u32[]{:S(2)}) copy-start(f32[2,4,800]{2,1,0:T(4,128)} %second_ref.1) | copy-start | bytes 76804

commit v3 on v2

--- a/solution.py
+++ b/solution.py
@@ -60,7 +60,10 @@
         ],
         compiler_params=PARAMS,
         cost_estimate=cost(2 * tokens * feats * rank, 2 * feats * (tokens + rank)),
-    )(inputs.T, projector)
+    )(
+        pltpu.with_memory_space_constraint(inputs.T, pltpu.HBM),
+        pltpu.with_memory_space_constraint(projector, pltpu.HBM),
+    )
 
 
 def halves(shape):

time: 83.4 us -> 81.9 us (0.982)
  local copies, waits for them, and re-layouts: 2.43 us -> 0.02 us
  Pallas kernels: 2.44 us -> 3.36 us
    unnamed x10 -> x6, local copies, waits for them, and re-layouts: 2.41 us -> 0.01 us
    pallas_call x1, Pallas kernels: 0.51 us -> 1.42 us  [low_parts(): pl.pallas_call(low_kernel, out_shape=(pltpu.VMEM((n_tensor, rank // n_ten...]
where the time goes in v3:
time: 81.9 us; the launch traced here: 81.6 us
  blocking collectives  77.6 us (95%)
  Pallas kernels  3.36 us (4%)
    all_to_all x4, blocking collectives, exchange(): return lax.all_to_all(blocks, axis, 0, 0)  77.6 us

profile of v3, /device:TPU:64, one launch (start us, length us, event | category | flops | bytes accessed | tf_op | source)
XLA Modules:
  0.0 81.6 jit_solution(1946353367731153552)
XLA Ops:
  0.6 0.0 copy-start
  0.6 1.4 %shard_map.76 = (bf16[16,8,512]{2,1,0:T(8,128)(2,1)S(1)}, bf16[160,128]{1,0:T(8,128)(2,1)S(1)}) custom-call(bf16[320,512]{1,0:T(8,128)(2,1)} %bitcast.7, bf16[5120,128]{1,0:T(8,128)(2,1)} %p_ref.1), custom_call_target="tpu_custom_call" | custom-call | flops 41943040 | bytes 409600 | tf_op jit(solution)/shard_map/pallas_call | solution.py:48
  2.1 15.7 %all_to_all.20 = bf16[16,8,512]{2,1,0:T(8,128)(2,1)S(1)} all-to-all(bf16[16,8,512]{2,1,0:T(8,128)(2,1)S(1)} %get-tuple-element.9), channel_id=1, replica_groups=mesh['dp'=32,'tensor'=16] {'tensor'}, dimensions={0} | all-to-all | bytes 262144 | tf_op jit(solution)/shard_map/all_to_all | solution.py:16
  17.9 11.6 %all_to_all.21.low_ref = bf16[16,8,512]{2,1,0:T(8,128)(2,1)S(1)} all-to-all(bf16[16,8,512]{2,1,0:T(8,128)(2,1)S(1)} %broadcast_in_dim.2), channel_id=1, replica_groups=mesh['dp'=32,'tensor'=16] {'tensor'}, dimensions={0} | all-to-all | bytes 262144 | tf_op jit(solution)/shard_map/all_to_all | solution.py:16
  29.5 0.0 copy-start.1
  29.5 0.0 copy-start.2
  29.5 0.0 copy-done
  29.5 0.7 shard_map.77
  30.2 29.5 %all_to_all.22.parts_ref = bf16[32,8,800]{2,1,0:T(8,128)(2,1)S(1)} all-to-all(bf16[32,8,800]{2,1,0:T(8,128)(2,1)S(1)} %bitcast.5), channel_id=1, replica_groups=mesh['dp'=32,'tensor'=16] {'dp'}, dimensions={0} | all-to-all | bytes 819200 | tf_op jit(solution)/shard_map/all_to_all | solution.py:16
  59.7 0.0 copy-done.1
  59.7 0.0 copy-done.2
  59.7 0.1 shard_map.78
  59.8 20.7 %all_to_all.23 = bf16[32,8,800]{2,1,0:T(8,128)(2,1)S(1)} all-to-all(bf16[32,8,800]{2,1,0:T(8,128)(2,1)S(1)} %get-tuple-element.10), channel_id=1, replica_groups=mesh['dp'=32,'tensor'=16] {'dp'}, dimensions={0} | all-to-all | bytes 819200 | tf_op jit(solution)/shard_map/all_to_all | solution.py:16
  80.5 1.1 %shard_map.79 = (bf16[2,160,800]{2,1,0:T(8,128)(2,1)}, f32[2,4,800]{2,1,0:T(4,128)}, f32[2,4,800]{2,1,0:T(4,128)}) custom-call(bf16[160,128]{1,0:T(8,128)(2,1)S(1)} %get-tuple-element.8.rows_ref, bf16[16,2,8,800]{3,2,1,0:T(8,128)(2,1)S(1)} %bitcast.4, f32[2,4,800]{2,1,0:T(4,128)S(1)} %get-tuple-element.11.first_ref, ...), custom_call_target="tpu_custom_call" | custom-call | flops 65536000 | bytes 512000 | tf_op jit(solution)/shard_map/pallas_call | solution.py:164
  (2 shorter events, 0.0 us)
Async XLA Ops:
  0.6 28.8 %copy-start = (bf16[2,512,800]{1,2,0:T(8,128)(2,1)S(1)}, bf16[2,512,800]{1,2,0:T(8,128)(2,1)}, u32[]{:S(2)}) copy-start(bf16[2,512,800]{1,2,0:T(8,128)(2,1)} %param.6) | copy-start | bytes 4915204
  29.5 30.2 %copy-start.1 = (f32[2,4,800]{2,1,0:T(4,128)S(1)}, f32[2,4,800]{2,1,0:T(4,128)}, u32[]{:S(2)}) copy-start(f32[2,4,800]{2,1,0:T(4,128)} %first_ref.1) | copy-start | bytes 76804
  29.5 30.2 %copy-start.2 = (f32[2,4,800]{2,1,0:T(4,128)S(1)}, f32[2,4,800]{2,1,0:T(4,128)}, u32[]{:S(2)}) copy-start(f32[2,4,800]{2,1,0:T(4,128)} %second_ref.1) | copy-start | bytes 76804

commit v4 on v3

--- a/solution.py
+++ b/solution.py
@@ -8,22 +8,44 @@
 FIRST_FIX = 1.0 - 0.9**10
 SECOND_FIX = 1.0 - 0.999**10
 PARAMS = pltpu.CompilerParams(vmem_limit_bytes=16 * 1024 * 1024)
+CHIPS_Z = 8
+CORES = 2
+SMEM = pl.BlockSpec(memory_space=pltpu.SMEM)
 VMEM = pl.BlockSpec(memory_space=pltpu.VMEM)
 HBM = pl.BlockSpec(memory_space=pltpu.HBM)
 
 
-def exchange(blocks, axis):
-    return lax.all_to_all(blocks, axis, 0, 0)
+def exchange(blocks, axis, groups=None):
+    return lax.all_to_all(blocks, axis, 0, 0, axis_index_groups=groups)
+
+
+def rows_sum(parts):
+    return jnp.sum(parts.astype(jnp.float32), axis=0)
+
+
+def scatter_at_once(sent):
+    return rows_sum(exchange(sent, "dp"))
+
+
+def scatter_by_axis(sent):
+    n_dp, height, columns = sent.shape
+    n_x = n_dp // CHIPS_Z
+    lines = [[x * CHIPS_Z + z for x in range(n_x)] for z in range(CHIPS_Z)]
+    planes = [[x * CHIPS_Z + z for z in range(CHIPS_Z)] for x in range(n_x)]
+    along_x = exchange(sent.reshape(n_x, CHIPS_Z * height, columns), "dp", lines)
+    own_plane = rows_sum(along_x).astype(sent.dtype).reshape(CHIPS_Z, height, columns)
+    return rows_sum(exchange(own_plane, "dp", planes))
 
 
 def cost(flops, nbytes):
     return pl.CostEstimate(flops=flops, bytes_accessed=nbytes, transcendentals=0)
 
 
-def low_kernel(x_ref, p_ref, parts_ref, rows_ref, x_buf, p_buf, sems):
+def low_kernel(first_core_ref, x_ref, p_ref, parts_ref, rows_ref, x_buf, p_buf, sems):
     n, height, tokens = parts_ref.shape
     feats, out_rows = x_ref.shape[0], rows_ref.shape[0]
-    own = pl.multiple_of(lax.axis_index("tensor") * feats, 16)
+    chip = lax.axis_index("tensor") // CORES
+    own = pl.multiple_of((chip * CORES + 1 - first_core_ref[0]) * feats, 16)
     block = pl.multiple_of(lax.axis_index("dp") * out_rows, 16)
     copies = (
         pltpu.make_async_copy(p_ref.at[pl.ds(own, feats)], p_buf, sems.at[0]),
@@ -41,7 +63,7 @@
     copies[2].wait()
 
 
-def low_parts(inputs, projector, n_tensor, n_dp):
+def low_parts(first_core, inputs, projector, n_tensor, n_dp):
     tokens, feats = inputs.shape
     width, rank = projector.shape
     bf16 = jnp.bfloat16
@@ -51,7 +73,7 @@
             pltpu.VMEM((n_tensor, rank // n_tensor, tokens), bf16),
             pltpu.VMEM((width // n_dp, rank), bf16),
         ),
-        in_specs=[HBM, HBM],
+        in_specs=[SMEM, HBM, HBM],
         out_specs=[VMEM, VMEM],
         scratch_shapes=[
             pltpu.VMEM((feats, tokens), bf16),
@@ -61,9 +83,26 @@
         compiler_params=PARAMS,
         cost_estimate=cost(2 * tokens * feats * rank, 2 * feats * (tokens + rank)),
     )(
+        first_core.astype(jnp.int32).reshape(1),
         pltpu.with_memory_space_constraint(inputs.T, pltpu.HBM),
         pltpu.with_memory_space_constraint(projector, pltpu.HBM),
     )
+
+
+def spread_kernel(parts_ref, out_ref):
+    own = jnp.sum(parts_ref[...].astype(jnp.float32), axis=0).astype(out_ref.dtype)
+    out_ref[...] = jnp.broadcast_to(own[None], out_ref.shape)
+
+
+def spread(parts):
+    return pl.pallas_call(
+        spread_kernel,
+        out_shape=pltpu.VMEM(parts.shape, parts.dtype),
+        in_specs=[VMEM],
+        out_specs=VMEM,
+        compiler_params=PARAMS,
+        cost_estimate=cost(parts.size, 4 * parts.size),
+    )(parts)
 
 
 def halves(shape):
@@ -99,12 +138,11 @@
     )(low, grads)
 
 
-def adam_kernel(parts_ref, first_ref, second_ref, out_ref, new_first_ref, new_second_ref):
-    own = jnp.sum(parts_ref[...].astype(jnp.float32), axis=0)
+def adam_kernel(own_ref, first_ref, second_ref, out_ref, new_first_ref, new_second_ref):
     n_grads, height, _ = first_ref.shape
     direction = []
     for k in range(n_grads):
-        projected = own[k * height : (k + 1) * height]
+        projected = own_ref[k * height : (k + 1) * height]
         first = 0.9 * first_ref[k] + 0.1 * projected
         second = 0.999 * second_ref[k] + 0.001 * projected * projected
         new_first_ref[k] = first
@@ -114,19 +152,19 @@
     out_ref[...] = jnp.broadcast_to(direction[None], out_ref.shape)
 
 
-def adam(parts, first, second):
+def adam(own, first, second, n_dp):
     return pl.pallas_call(
         adam_kernel,
         out_shape=(
-            pltpu.VMEM(parts.shape, jnp.bfloat16),
+            pltpu.VMEM((n_dp, *own.shape), jnp.bfloat16),
             pltpu.VMEM(first.shape, jnp.float32),
             pltpu.VMEM(second.shape, jnp.float32),
         ),
         in_specs=[VMEM] * 3,
         out_specs=[VMEM] * 3,
         compiler_params=PARAMS,
-        cost_estimate=cost(parts.size, 4 * parts.size),
-    )(parts, first, second)
+        cost_estimate=cost(20 * own.size, 2 * n_dp * own.size),
+    )(own, first, second)
 
 
 def expand_kernel(
@@ -179,13 +217,17 @@
 def per_device(inputs, out_grads, projector, first_moment, second_moment):
     n_dp, n_tensor = lax.axis_size("dp"), lax.axis_size("tensor")
     columns = out_grads.shape[2]
-    parts, rows = low_parts(inputs, projector, n_tensor, n_dp)
-    parts = exchange(parts, "tensor")
-    own_low = jnp.sum(parts.astype(jnp.float32), axis=0).astype(jnp.bfloat16)
-    low = exchange(jnp.broadcast_to(own_low[None], parts.shape), "tensor")
+    first_core = lax.axis_index("tensor") % CORES == 0
+    parts, rows = low_parts(first_core, inputs, projector, n_tensor, n_dp)
+    low = exchange(spread(exchange(parts, "tensor")), "tensor")
     sent = project(low, out_grads.transpose(0, 2, 1))
-    received = exchange(sent.reshape(n_dp, -1, columns), "dp")
-    direction, new_first, new_second = adam(received, first_moment, second_moment)
+    own = lax.cond(
+        first_core,
+        scatter_by_axis,
+        scatter_at_once,
+        sent.reshape(n_dp, -1, columns),
+    )
+    direction, new_first, new_second = adam(own, first_moment, second_moment, n_dp)
     every = exchange(direction, "dp").reshape(sent.shape)
     return expand(rows, every, new_first, new_second)
 

time: 81.9 us -> 78.7 us (0.961)
  blocking collectives: 77.6 us -> 74.2 us
    all_to_all x4 -> x5, blocking collectives: 77.6 us -> 74.2 us  [exchange(): return lax.all_to_all(blocks, axis, 0, 0, axis_index_groups=groups)]
where the time goes in v4:
time: 78.7 us; the launch traced here: 78.4 us
  blocking collectives  74.2 us (94%)
  Pallas kernels  3.33 us (4%)
    all_to_all x5, blocking collectives, exchange(): return lax.all_to_all(blocks, axis, 0, 0, axis_index_groups=groups)  74.2 us

profile of v4, /device:TPU:64, one launch (start us, length us, event | category | flops | bytes accessed | tf_op | source)
XLA Modules:
  0.0 78.4 jit_solution(14029269483430551101)
XLA Ops:
  0.6 0.0 copy-start
  0.7 1.4 %shard_map.76 = (bf16[16,8,512]{2,1,0:T(8,128)(2,1)S(1)}, bf16[160,128]{1,0:T(8,128)(2,1)S(1)}) custom-call(s32[1]{0:T(128)} %bitcast.3.first_core_ref, bf16[320,512]{1,0:T(8,128)(2,1)} %bitcast.12, bf16[5120,128]{1,0:T(8,128)(2,1)} %p_ref.1), custom_call_target="tpu_custom_call" | custom-call | flops 41943040 | bytes 409600 | tf_op jit(solution)/shard_map/pallas_call | solution.py:70
  2.1 15.7 %all_to_all.30.parts_ref = bf16[16,8,512]{2,1,0:T(8,128)(2,1)S(1)} all-to-all(bf16[16,8,512]{2,1,0:T(8,128)(2,1)S(1)} %get-tuple-element.15), channel_id=1, replica_groups=mesh['dp'=32,'tensor'=16] {'tensor'}, dimensions={0} | all-to-all | bytes 262144 | tf_op jit(solution)/shard_map/all_to_all | solution.py:19
  17.9 11.6 %all_to_all.31.low_ref = bf16[16,8,512]{2,1,0:T(8,128)(2,1)S(1)} all-to-all(bf16[16,8,512]{2,1,0:T(8,128)(2,1)S(1)} %shard_map.77), channel_id=1, replica_groups=mesh['dp'=32,'tensor'=16] {'tensor'}, dimensions={0} | all-to-all | bytes 262144 | tf_op jit(solution)/shard_map/all_to_all | solution.py:19
  29.4 0.0 copy-done
  29.5 0.7 shard_map.78
  30.2 0.0 copy-start.1
  30.2 0.0 copy-start.2
  30.2 29.5 %conditional.1 = (f32[8,800]{1,0:T(8,128)S(1)}) conditional(s32[]{:T(128)} %convert_element_type.12, bf16[16,2,8,800]{3,2,1,0:T(8,128)(2,1)S(1)} %shard_map.78, bf16[16,2,8,800]{3,2,1,0:T(8,128)(2,1)S(1)} %shard_map.78), branch_computations={%region_0.2_spmd, %region_2.5_spmd} | conditional | flops 403200 | bytes 1664010 | solution.py:224
  30.2 11.8 %all_to_all.28 = bf16[4,64,800]{2,1,0:T(8,128)(2,1)S(1)} all-to-all(bf16[4,64,800]{2,1,0:T(8,128)(2,1)S(1)} %bitcast.8), channel_id=1, replica_groups={{0,128,256,384},{16,144,272,400},{32,160,288,416},{48,176,304,432},{64,..., dimensions={0} | all-to-all | bytes 819200 | tf_op jit(solution)/shard_map/cond/branch_1_fun/all_to_all | solution.py:19
  42.0 0.1 reduce_sum.28
  42.1 17.5 %all_to_all.29 = bf16[8,8,800]{2,1,0:T(8,128)(2,1)S(1)} all-to-all(bf16[8,8,800]{2,1,0:T(8,128)(2,1)S(1)} %bitcast.11), channel_id=1, replica_groups={{0,16,32,48,64,80,96,112},{128,144,160,176,192,208,224,240},{256,272,28..., dimensions={0} | all-to-all | bytes 204800 | tf_op jit(solution)/shard_map/cond/branch_1_fun/all_to_all | solution.py:19
  59.7 0.0 copy-done.1
  59.7 0.0 copy-done.2
  59.7 0.1 shard_map.79
  59.8 17.5 %all_to_all.32 = bf16[32,8,800]{2,1,0:T(8,128)(2,1)S(1)} all-to-all(bf16[32,8,800]{2,1,0:T(8,128)(2,1)S(1)} %get-tuple-element.16), channel_id=1, replica_groups=mesh['dp'=32,'tensor'=16] {'dp'}, dimensions={0} | all-to-all | bytes 819200 | tf_op jit(solution)/shard_map/all_to_all | solution.py:19
  77.3 1.1 %shard_map.80 = (bf16[2,160,800]{2,1,0:T(8,128)(2,1)}, f32[2,4,800]{2,1,0:T(4,128)}, f32[2,4,800]{2,1,0:T(4,128)}) custom-call(bf16[160,128]{1,0:T(8,128)(2,1)S(1)} %get-tuple-element.14.rows_ref, bf16[16,2,8,800]{3,2,1,0:T(8,128)(2,1)S(1)} %bitcast.9, f32[2,4,800]{2,1,0:T(4,128)S(1)} %get-tuple-element.17.first_ref, ...), custom_call_target="tpu_custom_call" | custom-call | flops 65536000 | bytes 512000 | tf_op jit(solution)/shard_map/pallas_call | solution.py:202
  (2 shorter events, 0.0 us)
Async XLA Ops:
  0.6 28.8 %copy-start = (bf16[2,512,800]{1,2,0:T(8,128)(2,1)S(1)}, bf16[2,512,800]{1,2,0:T(8,128)(2,1)}, u32[]{:S(2)}) copy-start(bf16[2,512,800]{1,2,0:T(8,128)(2,1)} %param.8) | copy-start | bytes 4915204
  30.2 29.5 %copy-start.1 = (f32[2,4,800]{2,1,0:T(4,128)S(1)}, f32[2,4,800]{2,1,0:T(4,128)}, u32[]{:S(2)}) copy-start(f32[2,4,800]{2,1,0:T(4,128)} %first_ref.1) | copy-start | bytes 76804
  30.2 29.5 %copy-start.2 = (f32[2,4,800]{2,1,0:T(4,128)S(1)}, f32[2,4,800]{2,1,0:T(4,128)}, u32[]{:S(2)}) copy-start(f32[2,4,800]{2,1,0:T(4,128)} %second_ref.1) | copy-start | bytes 76804

commit v5 on v4

--- a/solution.py
+++ b/solution.py
@@ -9,6 +9,7 @@
 SECOND_FIX = 1.0 - 0.999**10
 PARAMS = pltpu.CompilerParams(vmem_limit_bytes=16 * 1024 * 1024)
 CHIPS_Z = 8
+HUB_X, HUB_Z, HUB_Y = 2, 4, 4
 CORES = 2
 SMEM = pl.BlockSpec(memory_space=pltpu.SMEM)
 VMEM = pl.BlockSpec(memory_space=pltpu.VMEM)
@@ -19,19 +20,28 @@
     return lax.all_to_all(blocks, axis, 0, 0, axis_index_groups=groups)
 
 
+def dp_order(n_dp):
+    hub = HUB_X * CHIPS_Z + HUB_Z
+    return [[at ^ hub for at in range(n_dp)]]
+
+
+def tensor_order(n_tensor):
+    return [[at ^ (HUB_Y * CORES) for at in range(n_tensor)]]
+
+
 def rows_sum(parts):
     return jnp.sum(parts.astype(jnp.float32), axis=0)
 
 
 def scatter_at_once(sent):
-    return rows_sum(exchange(sent, "dp"))
+    return rows_sum(exchange(sent, "dp", dp_order(sent.shape[0])))
 
 
 def scatter_by_axis(sent):
     n_dp, height, columns = sent.shape
     n_x = n_dp // CHIPS_Z
-    lines = [[x * CHIPS_Z + z for x in range(n_x)] for z in range(CHIPS_Z)]
-    planes = [[x * CHIPS_Z + z for z in range(CHIPS_Z)] for x in range(n_x)]
+    lines = [[(x ^ HUB_X) * CHIPS_Z + z for x in range(n_x)] for z in range(CHIPS_Z)]
+    planes = [[x * CHIPS_Z + (z ^ HUB_Z) for z in range(CHIPS_Z)] for x in range(n_x)]
     along_x = exchange(sent.reshape(n_x, CHIPS_Z * height, columns), "dp", lines)
     own_plane = rows_sum(along_x).astype(sent.dtype).reshape(CHIPS_Z, height, columns)
     return rows_sum(exchange(own_plane, "dp", planes))
@@ -105,6 +115,10 @@
     )(parts)
 
 
+def pair_at(pair):
+    return pair ^ ((HUB_X * CHIPS_Z + HUB_Z) // 2)
+
+
 def halves(shape):
     return lax.broadcasted_iota(jnp.int32, shape, 1) < shape[1] // 2
 
@@ -121,8 +135,11 @@
     )
     upper = halves(gate.shape)
     turn = height // 2
-    out_ref[:, 0] = jnp.where(upper, gate, pltpu.roll(up, turn, 1)).astype(out_ref.dtype)
-    out_ref[:, 1] = jnp.where(upper, pltpu.roll(gate, turn, 1), up).astype(out_ref.dtype)
+    even = jnp.where(upper, gate, pltpu.roll(up, turn, 1)).astype(out_ref.dtype)
+    odd = jnp.where(upper, pltpu.roll(gate, turn, 1), up).astype(out_ref.dtype)
+    for pair in range(groups):
+        out_ref[pair_at(pair), 0] = even[pair]
+        out_ref[pair_at(pair), 1] = odd[pair]
 
 
 def project(low, grads):
@@ -177,8 +194,10 @@
     ]
     for copy in copies:
         copy.start()
-    even = dirs_ref[:, 0].astype(jnp.float32)
-    odd = dirs_ref[:, 1].astype(jnp.float32)
+    even, odd = (
+        jnp.stack([dirs_ref[pair_at(pair), half] for pair in range(pairs)]).astype(jnp.float32)
+        for half in range(2)
+    )
     upper = halves(even.shape)
     turn = height // 2
     ordered = (
@@ -219,7 +238,8 @@
     columns = out_grads.shape[2]
     first_core = lax.axis_index("tensor") % CORES == 0
     parts, rows = low_parts(first_core, inputs, projector, n_tensor, n_dp)
-    low = exchange(spread(exchange(parts, "tensor")), "tensor")
+    by_tensor = tensor_order(n_tensor)
+    low = exchange(spread(exchange(parts, "tensor", by_tensor)), "tensor", by_tensor)
     sent = project(low, out_grads.transpose(0, 2, 1))
     own = lax.cond(
         first_core,
@@ -228,7 +248,7 @@
         sent.reshape(n_dp, -1, columns),
     )
     direction, new_first, new_second = adam(own, first_moment, second_moment, n_dp)
-    every = exchange(direction, "dp").reshape(sent.shape)
+    every = exchange(direction, "dp", dp_order(n_dp)).reshape(sent.shape)
     return expand(rows, every, new_first, new_second)
 
 

time: 78.7 us -> 74 us (0.940)
  the two profiles are of different devices: /device:TPU:64 before, /device:TPU:6 now
where the time goes in v5:
time: 74 us; the launch traced here: 73.7 us
  blocking collectives  69.5 us (94%)
  Pallas kernels  3.34 us (5%)
    all_to_all x5, blocking collectives, exchange(): return lax.all_to_all(blocks, axis, 0, 0, axis_index_groups=groups)  69.5 us

profile of v5, /device:TPU:6, one launch (start us, length us, event | category | flops | bytes accessed | tf_op | source)
XLA Modules:
  0.0 73.7 jit_solution(2187996463414762066)
XLA Ops:
  0.6 0.0 copy-start
  0.7 1.4 %shard_map.76 = (bf16[16,8,512]{2,1,0:T(8,128)(2,1)S(1)}, bf16[160,128]{1,0:T(8,128)(2,1)S(1)}) custom-call(s32[1]{0:T(128)} %bitcast.3.first_core_ref, bf16[320,512]{1,0:T(8,128)(2,1)} %bitcast.12, bf16[5120,128]{1,0:T(8,128)(2,1)} %p_ref.1), custom_call_target="tpu_custom_call" | custom-call | flops 41943040 | bytes 409600 | tf_op jit(solution)/shard_map/pallas_call | solution.py:80
  2.1 12.8 %all_to_all.30.parts_ref = bf16[16,8,512]{2,1,0:T(8,128)(2,1)S(1)} all-to-all(bf16[16,8,512]{2,1,0:T(8,128)(2,1)S(1)} %get-tuple-element.15), channel_id=1, replica_groups={{8,9,10,11,12,13,14,15,0,1,2,3,4,5,6,7},{24,25,26,27,28,29,30,31,16,17,..., dimensions={0} | all-to-all | bytes 262144 | tf_op jit(solution)/shard_map/all_to_all | solution.py:20
  14.9 11.6 %all_to_all.31.low_ref = bf16[16,8,512]{2,1,0:T(8,128)(2,1)S(1)} all-to-all(bf16[16,8,512]{2,1,0:T(8,128)(2,1)S(1)} %shard_map.77), channel_id=1, replica_groups={{8,9,10,11,12,13,14,15,0,1,2,3,4,5,6,7},{24,25,26,27,28,29,30,31,16,17,..., dimensions={0} | all-to-all | bytes 262144 | tf_op jit(solution)/shard_map/all_to_all | solution.py:20
  26.5 0.0 copy-done
  26.5 0.7 shard_map.78
  27.2 0.0 copy-start.1
  27.3 0.0 copy-start.2
  27.3 27.4 %conditional.1 = (f32[8,800]{1,0:T(8,128)S(1)}) conditional(s32[]{:T(128)} %convert_element_type.12, bf16[16,2,8,800]{3,2,1,0:T(8,128)(2,1)S(1)} %shard_map.78, bf16[16,2,8,800]{3,2,1,0:T(8,128)(2,1)S(1)} %shard_map.78), branch_computations={%region_0.2_spmd, %region_2.5_spmd} | conditional | flops 403200 | bytes 1664010 | solution.py:244
  27.3 13.1 %all_to_all.28 = bf16[4,64,800]{2,1,0:T(8,128)(2,1)S(1)} all-to-all(bf16[4,64,800]{2,1,0:T(8,128)(2,1)S(1)} %bitcast.8), channel_id=1, replica_groups={{256,384,0,128},{272,400,16,144},{288,416,32,160},{304,432,48,176},{320..., dimensions={0} | all-to-all | bytes 819200 | tf_op jit(solution)/shard_map/cond/branch_1_fun/all_to_all | solution.py:20
  40.4 0.1 reduce_sum.28
  40.5 14.1 %all_to_all.29 = bf16[8,8,800]{2,1,0:T(8,128)(2,1)S(1)} all-to-all(bf16[8,8,800]{2,1,0:T(8,128)(2,1)S(1)} %bitcast.11), channel_id=1, replica_groups={{64,80,96,112,0,16,32,48},{192,208,224,240,128,144,160,176},{320,336,35..., dimensions={0} | all-to-all | bytes 204800 | tf_op jit(solution)/shard_map/cond/branch_1_fun/all_to_all | solution.py:20
  54.6 0.0 copy-done.1
  54.7 0.0 copy-done.2
  54.7 0.1 shard_map.79
  54.7 17.8 %all_to_all.32 = bf16[32,8,800]{2,1,0:T(8,128)(2,1)S(1)} all-to-all(bf16[32,8,800]{2,1,0:T(8,128)(2,1)S(1)} %get-tuple-element.16), channel_id=1, replica_groups={{320,336,352,368,256,272,288,304,448,464,480,496,384,400,416,432,64,80,..., dimensions={0} | all-to-all | bytes 819200 | tf_op jit(solution)/shard_map/all_to_all | solution.py:20
  72.6 1.1 %shard_map.80 = (bf16[2,160,800]{2,1,0:T(8,128)(2,1)}, f32[2,4,800]{2,1,0:T(4,128)}, f32[2,4,800]{2,1,0:T(4,128)}) custom-call(bf16[160,128]{1,0:T(8,128)(2,1)S(1)} %get-tuple-element.14.rows_ref, bf16[16,2,8,800]{3,2,1,0:T(8,128)(2,1)S(1)} %bitcast.9, f32[2,4,800]{2,1,0:T(4,128)S(1)} %get-tuple-element.17.first_ref, ...), custom_call_target="tpu_custom_call" | custom-call | flops 65536000 | bytes 512000 | tf_op jit(solution)/shard_map/pallas_call | solution.py:221
  (2 shorter events, 0.0 us)
Async XLA Ops:
  0.6 25.9 %copy-start = (bf16[2,512,800]{1,2,0:T(8,128)(2,1)S(1)}, bf16[2,512,800]{1,2,0:T(8,128)(2,1)}, u32[]{:S(2)}) copy-start(bf16[2,512,800]{1,2,0:T(8,128)(2,1)} %param.8) | copy-start | bytes 4915204
  27.2 27.4 %copy-start.1 = (f32[2,4,800]{2,1,0:T(4,128)S(1)}, f32[2,4,800]{2,1,0:T(4,128)}, u32[]{:S(2)}) copy-start(f32[2,4,800]{2,1,0:T(4,128)} %first_ref.1) | copy-start | bytes 76804
  27.3 27.4 %copy-start.2 = (f32[2,4,800]{2,1,0:T(4,128)S(1)}, f32[2,4,800]{2,1,0:T(4,128)}, u32[]{:S(2)}) copy-start(f32[2,4,800]{2,1,0:T(4,128)} %second_ref.1) | copy-start | bytes 76804

commit v6 on v5

--- a/solution.py
+++ b/solution.py
@@ -9,7 +9,7 @@
 SECOND_FIX = 1.0 - 0.999**10
 PARAMS = pltpu.CompilerParams(vmem_limit_bytes=16 * 1024 * 1024)
 CHIPS_Z = 8
-HUB_X, HUB_Z, HUB_Y = 2, 4, 4
+LAST_X, LAST_Y, LAST_Z = 2, 4, 4
 CORES = 2
 SMEM = pl.BlockSpec(memory_space=pltpu.SMEM)
 VMEM = pl.BlockSpec(memory_space=pltpu.VMEM)
@@ -20,13 +20,20 @@
     return lax.all_to_all(blocks, axis, 0, 0, axis_index_groups=groups)
 
 
+def far_first(n, last):
+    steps = [0, n // 2] + [sign * far for far in range(n // 2 - 1, 0, -1) for sign in (-1, 1)]
+    return [(last + step) % n for step in steps]
+
+
 def dp_order(n_dp):
-    hub = HUB_X * CHIPS_Z + HUB_Z
-    return [[at ^ hub for at in range(n_dp)]]
+    n_x = n_dp // CHIPS_Z
+    return [x * CHIPS_Z + z for x in far_first(n_x, LAST_X) for z in far_first(CHIPS_Z, LAST_Z)]
 
 
 def tensor_order(n_tensor):
-    return [[at ^ (HUB_Y * CORES) for at in range(n_tensor)]]
+    chips = far_first(n_tensor // CORES, LAST_Y)
+    order = [chip * CORES + core for chip in chips for core in (1, 0)]
+    return order[:1] + order[2:] + order[1:2]
 
 
 def rows_sum(parts):
@@ -34,14 +41,14 @@
 
 
 def scatter_at_once(sent):
-    return rows_sum(exchange(sent, "dp", dp_order(sent.shape[0])))
+    return rows_sum(exchange(sent, "dp", [dp_order(sent.shape[0])]))
 
 
 def scatter_by_axis(sent):
     n_dp, height, columns = sent.shape
     n_x = n_dp // CHIPS_Z
-    lines = [[(x ^ HUB_X) * CHIPS_Z + z for x in range(n_x)] for z in range(CHIPS_Z)]
-    planes = [[x * CHIPS_Z + (z ^ HUB_Z) for z in range(CHIPS_Z)] for x in range(n_x)]
+    lines = [[x * CHIPS_Z + z for x in far_first(n_x, LAST_X)] for z in range(CHIPS_Z)]
+    planes = [[x * CHIPS_Z + z for z in far_first(CHIPS_Z, LAST_Z)] for x in range(n_x)]
     along_x = exchange(sent.reshape(n_x, CHIPS_Z * height, columns), "dp", lines)
     own_plane = rows_sum(along_x).astype(sent.dtype).reshape(CHIPS_Z, height, columns)
     return rows_sum(exchange(own_plane, "dp", planes))
@@ -115,10 +122,6 @@
     )(parts)
 
 
-def pair_at(pair):
-    return pair ^ ((HUB_X * CHIPS_Z + HUB_Z) // 2)
-
-
 def halves(shape):
     return lax.broadcasted_iota(jnp.int32, shape, 1) < shape[1] // 2
 
@@ -137,9 +140,10 @@
     turn = height // 2
     even = jnp.where(upper, gate, pltpu.roll(up, turn, 1)).astype(out_ref.dtype)
     odd = jnp.where(upper, pltpu.roll(gate, turn, 1), up).astype(out_ref.dtype)
+    order = dp_order(2 * groups)
     for pair in range(groups):
-        out_ref[pair_at(pair), 0] = even[pair]
-        out_ref[pair_at(pair), 1] = odd[pair]
+        out_ref[order.index(2 * pair)] = even[pair]
+        out_ref[order.index(2 * pair + 1)] = odd[pair]
 
 
 def project(low, grads):
@@ -147,7 +151,7 @@
     columns = grads.shape[1]
     return pl.pallas_call(
         project_kernel,
-        out_shape=pltpu.VMEM((groups, 2, height, columns), jnp.bfloat16),
+        out_shape=pltpu.VMEM((2 * groups, height, columns), jnp.bfloat16),
         in_specs=[VMEM, VMEM],
         out_specs=VMEM,
         compiler_params=PARAMS,
@@ -187,7 +191,8 @@
 def expand_kernel(
     rows_ref, dirs_ref, first_ref, second_ref, out_ref, new_first_ref, new_second_ref, buf, sems
 ):
-    pairs, _, height, columns = dirs_ref.shape
+    n_dp, height, columns = dirs_ref.shape
+    order = dp_order(n_dp)
     copies = [
         pltpu.make_async_copy(first_ref, new_first_ref, sems.at[2]),
         pltpu.make_async_copy(second_ref, new_second_ref, sems.at[3]),
@@ -195,7 +200,7 @@
     for copy in copies:
         copy.start()
     even, odd = (
-        jnp.stack([dirs_ref[pair_at(pair), half] for pair in range(pairs)]).astype(jnp.float32)
+        jnp.stack([dirs_ref[order.index(at)] for at in range(half, n_dp, 2)]).astype(jnp.float32)
         for half in range(2)
     )
     upper = halves(even.shape)
@@ -205,7 +210,7 @@
         jnp.where(upper, pltpu.roll(even, turn, 1), odd),
     )
     for k in range(2):
-        direction = ordered[k].astype(jnp.bfloat16).reshape(pairs * height, columns)
+        direction = ordered[k].astype(jnp.bfloat16).reshape(n_dp // 2 * height, columns)
         update = jnp.dot(rows_ref[...], direction, preferred_element_type=jnp.float32)
         buf[k] = update.astype(buf.dtype)
         copies.append(pltpu.make_async_copy(buf.at[k], out_ref.at[k], sems.at[k]))
@@ -235,20 +240,14 @@
 
 def per_device(inputs, out_grads, projector, first_moment, second_moment):
     n_dp, n_tensor = lax.axis_size("dp"), lax.axis_size("tensor")
-    columns = out_grads.shape[2]
     first_core = lax.axis_index("tensor") % CORES == 0
     parts, rows = low_parts(first_core, inputs, projector, n_tensor, n_dp)
-    by_tensor = tensor_order(n_tensor)
+    by_tensor = [tensor_order(n_tensor)]
     low = exchange(spread(exchange(parts, "tensor", by_tensor)), "tensor", by_tensor)
     sent = project(low, out_grads.transpose(0, 2, 1))
-    own = lax.cond(
-        first_core,
-        scatter_by_axis,
-        scatter_at_once,
-        sent.reshape(n_dp, -1, columns),
-    )
+    own = lax.cond(first_core, scatter_by_axis, scatter_at_once, sent)
     direction, new_first, new_second = adam(own, first_moment, second_moment, n_dp)
-    every = exchange(direction, "dp", dp_order(n_dp)).reshape(sent.shape)
+    every = exchange(direction, "dp", [dp_order(n_dp)])
     return expand(rows, every, new_first, new_second)
 
 

time: 74 us -> 72.7 us (0.982); the launches traced: 73.7 us -> 71.3 us
  blocking collectives: 69.5 us -> 67.1 us
    all_to_all x5, blocking collectives: 69.5 us -> 67.1 us  [exchange(): return lax.all_to_all(blocks, axis, 0, 0, axis_index_groups=groups)]
where the time goes in v6:
time: 72.7 us; the launch traced here: 71.3 us
  blocking collectives  67.1 us (92%)
  Pallas kernels  3.33 us (5%)
    all_to_all x5, blocking collectives, exchange(): return lax.all_to_all(blocks, axis, 0, 0, axis_index_groups=groups)  67.1 us

profile of v6, /device:TPU:6, one launch (start us, length us, event | category | flops | bytes accessed | tf_op | source)
XLA Modules:
  0.0 71.3 jit_solution(733661448813963519)
XLA Ops:
  0.6 0.0 copy-start
  0.7 1.4 %shard_map.76 = (bf16[16,8,512]{2,1,0:T(8,128)(2,1)S(1)}, bf16[160,128]{1,0:T(8,128)(2,1)S(1)}) custom-call(s32[1]{0:T(128)} %bitcast.2.first_core_ref, bf16[320,512]{1,0:T(8,128)(2,1)} %bitcast.8, bf16[5120,128]{1,0:T(8,128)(2,1)} %p_ref.1), custom_call_target="tpu_custom_call" | custom-call | flops 41943040 | bytes 409600 | tf_op jit(solution)/shard_map/pallas_call | solution.py:87
  2.1 11.5 %all_to_all.30.parts_ref = bf16[16,8,512]{2,1,0:T(8,128)(2,1)S(1)} all-to-all(bf16[16,8,512]{2,1,0:T(8,128)(2,1)S(1)} %get-tuple-element.14), channel_id=1, replica_groups={{9,1,0,3,2,15,14,5,4,13,12,7,6,11,10,8},{25,17,16,19,18,31,30,21,20,29,..., dimensions={0} | all-to-all | bytes 262144 | tf_op jit(solution)/shard_map/all_to_all | solution.py:20
  13.6 11.2 %all_to_all.31.low_ref = bf16[16,8,512]{2,1,0:T(8,128)(2,1)S(1)} all-to-all(bf16[16,8,512]{2,1,0:T(8,128)(2,1)S(1)} %shard_map.77), channel_id=1, replica_groups={{9,1,0,3,2,15,14,5,4,13,12,7,6,11,10,8},{25,17,16,19,18,31,30,21,20,29,..., dimensions={0} | all-to-all | bytes 262144 | tf_op jit(solution)/shard_map/all_to_all | solution.py:20
  24.9 0.0 copy-done
  24.9 0.7 shard_map.78
  25.6 0.0 copy-start.1
  25.6 0.0 copy-start.2
  25.6 27.3 %conditional.1 = (f32[8,800]{1,0:T(8,128)S(1)}) conditional(s32[]{:T(128)} %convert_element_type.12, bf16[32,8,800]{2,1,0:T(8,128)(2,1)S(1)} %shard_map.78, bf16[32,8,800]{2,1,0:T(8,128)(2,1)S(1)} %shard_map.78), branch_computations={%region_0.2_spmd, %region_2.5_spmd} | conditional | flops 403200 | bytes 1664010 | solution.py:248
  25.6 13.4 %all_to_all.28 = bf16[4,64,800]{2,1,0:T(8,128)(2,1)S(1)} all-to-all(bf16[4,64,800]{2,1,0:T(8,128)(2,1)S(1)} %bitcast.5), channel_id=1, replica_groups={{256,0,128,384},{272,16,144,400},{288,32,160,416},{304,48,176,432},{320..., dimensions={0} | all-to-all | bytes 819200 | tf_op jit(solution)/shard_map/cond/branch_1_fun/all_to_all | solution.py:20
  39.0 0.1 reduce_sum.28
  39.1 13.8 %all_to_all.29 = bf16[8,8,800]{2,1,0:T(8,128)(2,1)S(1)} all-to-all(bf16[8,8,800]{2,1,0:T(8,128)(2,1)S(1)} %bitcast.7), channel_id=1, replica_groups={{64,0,16,112,32,96,48,80},{192,128,144,240,160,224,176,208},{320,256,27..., dimensions={0} | all-to-all | bytes 204800 | tf_op jit(solution)/shard_map/cond/branch_1_fun/all_to_all | solution.py:20
  52.9 0.0 copy-done.1
  52.9 0.0 copy-done.2
  52.9 0.1 shard_map.79
  53.0 17.2 %all_to_all.32.dirs_ref = bf16[32,8,800]{2,1,0:T(8,128)(2,1)S(1)} all-to-all(bf16[32,8,800]{2,1,0:T(8,128)(2,1)S(1)} %get-tuple-element.15), channel_id=1, replica_groups={{320,256,272,368,288,352,304,336,64,0,16,112,32,96,48,80,192,128,144,24..., dimensions={0} | all-to-all | bytes 819200 | tf_op jit(solution)/shard_map/all_to_all | solution.py:20
  70.2 1.1 %shard_map.80 = (bf16[2,160,800]{2,1,0:T(8,128)(2,1)}, f32[2,4,800]{2,1,0:T(4,128)}, f32[2,4,800]{2,1,0:T(4,128)}) custom-call(bf16[160,128]{1,0:T(8,128)(2,1)S(1)} %get-tuple-element.13.rows_ref, bf16[32,8,800]{2,1,0:T(8,128)(2,1)S(1)} %all_to_all.32.dirs_ref, f32[2,4,800]{2,1,0:T(4,128)S(1)} %get-tuple-element.16.first_ref, ...), custom_call_target="tpu_custom_call" | custom-call | flops 65536000 | bytes 512000 | tf_op jit(solution)/shard_map/pallas_call | solution.py:226
  (2 shorter events, 0.0 us)
Async XLA Ops:
  0.6 24.2 %copy-start = (bf16[2,512,800]{1,2,0:T(8,128)(2,1)S(1)}, bf16[2,512,800]{1,2,0:T(8,128)(2,1)}, u32[]{:S(2)}) copy-start(bf16[2,512,800]{1,2,0:T(8,128)(2,1)} %param.8) | copy-start | bytes 4915204
  25.6 27.3 %copy-start.1 = (f32[2,4,800]{2,1,0:T(4,128)S(1)}, f32[2,4,800]{2,1,0:T(4,128)}, u32[]{:S(2)}) copy-start(f32[2,4,800]{2,1,0:T(4,128)} %first_ref.1) | copy-start | bytes 76804
  25.6 27.3 %copy-start.2 = (f32[2,4,800]{2,1,0:T(4,128)S(1)}, f32[2,4,800]{2,1,0:T(4,128)}, u32[]{:S(2)}) copy-start(f32[2,4,800]{2,1,0:T(4,128)} %second_ref.1) | copy-start | bytes 76804

commit v7 on v6

--- a/solution.py
+++ b/solution.py
@@ -45,13 +45,12 @@
 
 
 def scatter_by_axis(sent):
-    n_dp, height, columns = sent.shape
+    n_dp, own_rank, width = sent.shape
     n_x = n_dp // CHIPS_Z
     lines = [[x * CHIPS_Z + z for x in far_first(n_x, LAST_X)] for z in range(CHIPS_Z)]
     planes = [[x * CHIPS_Z + z for z in far_first(CHIPS_Z, LAST_Z)] for x in range(n_x)]
-    along_x = exchange(sent.reshape(n_x, CHIPS_Z * height, columns), "dp", lines)
-    own_plane = rows_sum(along_x).astype(sent.dtype).reshape(CHIPS_Z, height, columns)
-    return rows_sum(exchange(own_plane, "dp", planes))
+    along_x = exchange(sent.reshape(n_x, CHIPS_Z, own_rank, width), "dp", lines)
+    return rows_sum(exchange(rows_sum(along_x).astype(sent.dtype), "dp", planes))
 
 
 def cost(flops, nbytes):
@@ -122,54 +121,47 @@
     )(parts)
 
 
-def halves(shape):
-    return lax.broadcasted_iota(jnp.int32, shape, 1) < shape[1] // 2
-
-
 def project_kernel(low_ref, grads_ref, out_ref):
     groups, height, tokens = low_ref.shape
-    columns = grads_ref.shape[1]
-    low = low_ref[...].reshape(groups * height, tokens)
-    gate, up = (
-        lax.dot_general(
-            low, grads_ref[k], (((1,), (1,)), ((), ())), preferred_element_type=jnp.float32
-        ).reshape(groups, height, columns)
-        for k in range(2)
-    )
-    upper = halves(gate.shape)
-    turn = height // 2
-    even = jnp.where(upper, gate, pltpu.roll(up, turn, 1)).astype(out_ref.dtype)
-    odd = jnp.where(upper, pltpu.roll(gate, turn, 1), up).astype(out_ref.dtype)
-    order = dp_order(2 * groups)
-    for pair in range(groups):
-        out_ref[order.index(2 * pair)] = even[pair]
-        out_ref[order.index(2 * pair + 1)] = odd[pair]
-
-
-def project(low, grads):
+    n_grads, columns, _ = grads_ref.shape
+    n_dp, own_rank, _ = out_ref.shape
+    projected = lax.dot_general(
+        low_ref[...].reshape(groups * height, tokens),
+        grads_ref[...].reshape(n_grads * columns, tokens),
+        (((1,), (1,)), ((), ())),
+        preferred_element_type=jnp.float32,
+    )
+    order = dp_order(n_dp)
+    for at in range(n_dp):
+        rows = projected[at * own_rank : (at + 1) * own_rank]
+        out_ref[order.index(at)] = rows.astype(out_ref.dtype)
+
+
+def project(low, grads, n_dp):
     groups, height, tokens = low.shape
-    columns = grads.shape[1]
+    n_grads, columns, _ = grads.shape
+    rank = groups * height
     return pl.pallas_call(
         project_kernel,
-        out_shape=pltpu.VMEM((2 * groups, height, columns), jnp.bfloat16),
+        out_shape=pltpu.VMEM((n_dp, rank // n_dp, n_grads * columns), jnp.bfloat16),
         in_specs=[VMEM, VMEM],
         out_specs=VMEM,
         compiler_params=PARAMS,
-        cost_estimate=cost(4 * groups * height * tokens * columns, 4 * tokens * columns),
+        cost_estimate=cost(2 * rank * tokens * n_grads * columns, 4 * tokens * columns),
     )(low, grads)
 
 
 def adam_kernel(own_ref, first_ref, second_ref, out_ref, new_first_ref, new_second_ref):
-    n_grads, height, _ = first_ref.shape
+    n_grads, _, columns = first_ref.shape
     direction = []
     for k in range(n_grads):
-        projected = own_ref[k * height : (k + 1) * height]
+        projected = own_ref[:, k * columns : (k + 1) * columns]
         first = 0.9 * first_ref[k] + 0.1 * projected
         second = 0.999 * second_ref[k] + 0.001 * projected * projected
         new_first_ref[k] = first
         new_second_ref[k] = second
         direction.append(first / FIRST_FIX / (jnp.sqrt(second / SECOND_FIX) + 1e-08))
-    direction = jnp.concatenate(direction, axis=0).astype(out_ref.dtype)
+    direction = jnp.concatenate(direction, axis=1).astype(out_ref.dtype)
     out_ref[...] = jnp.broadcast_to(direction[None], out_ref.shape)
 
 
@@ -191,7 +183,7 @@
 def expand_kernel(
     rows_ref, dirs_ref, first_ref, second_ref, out_ref, new_first_ref, new_second_ref, buf, sems
 ):
-    n_dp, height, columns = dirs_ref.shape
+    n_dp, columns = dirs_ref.shape[0], out_ref.shape[2]
     order = dp_order(n_dp)
     copies = [
         pltpu.make_async_copy(first_ref, new_first_ref, sems.at[2]),
@@ -199,20 +191,13 @@
     ]
     for copy in copies:
         copy.start()
-    even, odd = (
-        jnp.stack([dirs_ref[order.index(at)] for at in range(half, n_dp, 2)]).astype(jnp.float32)
-        for half in range(2)
-    )
-    upper = halves(even.shape)
-    turn = height // 2
-    ordered = (
-        jnp.where(upper, even, pltpu.roll(odd, turn, 1)),
-        jnp.where(upper, pltpu.roll(even, turn, 1), odd),
-    )
+    direction = jnp.concatenate(
+        [dirs_ref[order.index(at)].astype(jnp.float32) for at in range(n_dp)], axis=0
+    ).astype(jnp.bfloat16)
+    update = jnp.dot(rows_ref[...], direction, preferred_element_type=jnp.float32)
+    update = update.astype(buf.dtype)
     for k in range(2):
-        direction = ordered[k].astype(jnp.bfloat16).reshape(n_dp // 2 * height, columns)
-        update = jnp.dot(rows_ref[...], direction, preferred_element_type=jnp.float32)
-        buf[k] = update.astype(buf.dtype)
+        buf[k] = update[:, k * columns : (k + 1) * columns]
         copies.append(pltpu.make_async_copy(buf.at[k], out_ref.at[k], sems.at[k]))
         copies[-1].start()
     for copy in copies:
@@ -221,7 +206,7 @@
 
 def expand(rows, dirs, first, second):
     out_rows, rank = rows.shape
-    columns = dirs.shape[-1]
+    columns = dirs.shape[-1] // 2
     shape = (2, out_rows, columns)
     return pl.pallas_call(
         expand_kernel,
@@ -244,7 +229,7 @@
     parts, rows = low_parts(first_core, inputs, projector, n_tensor, n_dp)
     by_tensor = [tensor_order(n_tensor)]
     low = exchange(spread(exchange(parts, "tensor", by_tensor)), "tensor", by_tensor)
-    sent = project(low, out_grads.transpose(0, 2, 1))
+    sent = project(low, out_grads.transpose(0, 2, 1), n_dp)
     own = lax.cond(first_core, scatter_by_axis, scatter_at_once, sent)
     direction, new_first, new_second = adam(own, first_moment, second_moment, n_dp)
     every = exchange(direction, "dp", [dp_order(n_dp)])

time: 72.7 us -> 72.4 us (level)
    all_to_all x5, blocking collectives: 67.1 us -> 66.4 us  [exchange(): return lax.all_to_all(blocks, axis, 0, 0, axis_index_groups=groups)]
where the time goes in v7:
time: 72.4 us; the launch traced here: 70.9 us
  blocking collectives  66.4 us (92%)
  Pallas kernels  3.47 us (5%)
    all_to_all x5, blocking collectives, exchange(): return lax.all_to_all(blocks, axis, 0, 0, axis_index_groups=groups)  66.4 us

profile of v7, /device:TPU:6, one launch (start us, length us, event | category | flops | bytes accessed | tf_op | source)
XLA Modules:
  0.0 70.9 jit_solution(16235968537208119267)
XLA Ops:
  0.6 0.0 copy-start
  0.7 1.4 %shard_map.76 = (bf16[16,8,512]{2,1,0:T(8,128)(2,1)S(1)}, bf16[160,128]{1,0:T(8,128)(2,1)S(1)}) custom-call(s32[1]{0:T(128)} %bitcast.1.first_core_ref, bf16[320,512]{1,0:T(8,128)(2,1)} %bitcast.6, bf16[5120,128]{1,0:T(8,128)(2,1)} %p_ref.1), custom_call_target="tpu_custom_call" | custom-call | flops 41943040 | bytes 409600 | tf_op jit(solution)/shard_map/pallas_call | solution.py:86
  2.1 11.5 %all_to_all.30.parts_ref = bf16[16,8,512]{2,1,0:T(8,128)(2,1)S(1)} all-to-all(bf16[16,8,512]{2,1,0:T(8,128)(2,1)S(1)} %get-tuple-element.14), channel_id=1, replica_groups={{9,1,0,3,2,15,14,5,4,13,12,7,6,11,10,8},{25,17,16,19,18,31,30,21,20,29,..., dimensions={0} | all-to-all | bytes 262144 | tf_op jit(solution)/shard_map/all_to_all | solution.py:20
  13.6 11.2 %all_to_all.31.low_ref = bf16[16,8,512]{2,1,0:T(8,128)(2,1)S(1)} all-to-all(bf16[16,8,512]{2,1,0:T(8,128)(2,1)S(1)} %shard_map.77), channel_id=1, replica_groups={{9,1,0,3,2,15,14,5,4,13,12,7,6,11,10,8},{25,17,16,19,18,31,30,21,20,29,..., dimensions={0} | all-to-all | bytes 262144 | tf_op jit(solution)/shard_map/all_to_all | solution.py:20
  24.9 0.0 copy-done
  24.9 0.7 shard_map.78
  25.5 0.0 copy-start.1
  25.5 0.0 copy-start.2
  25.6 27.0 %conditional.1 = (f32[4,1600]{1,0:T(4,128)S(1)}) conditional(s32[]{:T(128)} %convert_element_type.12, bf16[32,4,1600]{2,1,0:T(4,128)(2,1)S(1)} %shard_map.78, bf16[32,4,1600]{2,1,0:T(4,128)(2,1)S(1)} %shard_map.78), branch_computations={%region_0.2_spmd, %region_2.5_spmd} | conditional | flops 403200 | bytes 1664010 | solution.py:233
  25.6 13.2 %all_to_all.28 = bf16[4,8,4,1600]{3,2,1,0:T(4,128)(2,1)S(1)} all-to-all(bf16[4,8,4,1600]{3,2,1,0:T(4,128)(2,1)S(1)} %bitcast.4), channel_id=1, replica_groups={{256,0,128,384},{272,16,144,400},{288,32,160,416},{304,48,176,432},{320..., dimensions={0} | all-to-all | bytes 819200 | tf_op jit(solution)/shard_map/cond/branch_1_fun/all_to_all | solution.py:20
  38.8 0.3 reduce_sum.28
  39.1 13.5 %all_to_all.29 = bf16[8,4,1600]{2,1,0:T(4,128)(2,1)S(1)} all-to-all(bf16[8,4,1600]{2,1,0:T(4,128)(2,1)S(1)} %reduce_sum.28), channel_id=1, replica_groups={{64,0,16,112,32,96,48,80},{192,128,144,240,160,224,176,208},{320,256,27..., dimensions={0} | all-to-all | bytes 204800 | tf_op jit(solution)/shard_map/cond/branch_1_fun/all_to_all | solution.py:20
  52.5 0.1 convert_reduce_fusion.1
  52.6 0.0 copy-done.1
  52.6 0.0 copy-done.2
  52.6 0.2 shard_map.79
  52.8 17.0 %all_to_all.32.dirs_ref = bf16[32,4,1600]{2,1,0:T(4,128)(2,1)S(1)} all-to-all(bf16[32,4,1600]{2,1,0:T(4,128)(2,1)S(1)} %get-tuple-element.15), channel_id=1, replica_groups={{320,256,272,368,288,352,304,336,64,0,16,112,32,96,48,80,192,128,144,24..., dimensions={0} | all-to-all | bytes 819200 | tf_op jit(solution)/shard_map/all_to_all | solution.py:20
  69.8 1.2 %shard_map.80 = (bf16[2,160,800]{2,1,0:T(8,128)(2,1)}, f32[2,4,800]{2,1,0:T(4,128)}, f32[2,4,800]{2,1,0:T(4,128)}) custom-call(bf16[160,128]{1,0:T(8,128)(2,1)S(1)} %get-tuple-element.13.rows_ref, bf16[32,4,1600]{2,1,0:T(4,128)(2,1)S(1)} %all_to_all.32.dirs_ref, f32[2,4,800]{2,1,0:T(4,128)S(1)} %get-tuple-element.16.first_ref, ...), custom_call_target="tpu_custom_call" | custom-call | flops 65536000 | bytes 512000 | tf_op jit(solution)/shard_map/pallas_call | solution.py:211
  (1 shorter events, 0.0 us)
Async XLA Ops:
  0.6 24.2 %copy-start = (bf16[2,512,800]{1,2,0:T(8,128)(2,1)S(1)}, bf16[2,512,800]{1,2,0:T(8,128)(2,1)}, u32[]{:S(2)}) copy-start(bf16[2,512,800]{1,2,0:T(8,128)(2,1)} %param.8) | copy-start | bytes 4915204
  25.5 27.1 %copy-start.1 = (f32[2,4,800]{2,1,0:T(4,128)S(1)}, f32[2,4,800]{2,1,0:T(4,128)}, u32[]{:S(2)}) copy-start(f32[2,4,800]{2,1,0:T(4,128)} %first_ref.1) | copy-start | bytes 76804
  25.5 27.1 %copy-start.2 = (f32[2,4,800]{2,1,0:T(4,128)S(1)}, f32[2,4,800]{2,1,0:T(4,128)}, u32[]{:S(2)}) copy-start(f32[2,4,800]{2,1,0:T(4,128)} %second_ref.1) | copy-start | bytes 76804

commit v8 on v7

--- a/solution.py
+++ b/solution.py
@@ -50,7 +50,7 @@
     lines = [[x * CHIPS_Z + z for x in far_first(n_x, LAST_X)] for z in range(CHIPS_Z)]
     planes = [[x * CHIPS_Z + z for z in far_first(CHIPS_Z, LAST_Z)] for x in range(n_x)]
     along_x = exchange(sent.reshape(n_x, CHIPS_Z, own_rank, width), "dp", lines)
-    return rows_sum(exchange(rows_sum(along_x).astype(sent.dtype), "dp", planes))
+    return rows_sum(exchange(total(along_x), "dp", planes))
 
 
 def cost(flops, nbytes):
@@ -103,6 +103,21 @@
         pltpu.with_memory_space_constraint(inputs.T, pltpu.HBM),
         pltpu.with_memory_space_constraint(projector, pltpu.HBM),
     )
+
+
+def total_kernel(parts_ref, out_ref):
+    out_ref[...] = rows_sum(parts_ref[...]).astype(out_ref.dtype)
+
+
+def total(parts):
+    return pl.pallas_call(
+        total_kernel,
+        out_shape=pltpu.VMEM(parts.shape[1:], parts.dtype),
+        in_specs=[VMEM],
+        out_specs=VMEM,
+        compiler_params=PARAMS,
+        cost_estimate=cost(parts.size, 3 * parts.size),
+    )(parts)
 
 
 def spread_kernel(parts_ref, out_ref):

time: 72.4 us -> 72.3 us (level)
  no operation moved by 1% of the time
where the time goes in v8:
time: 72.3 us; the launch traced here: 70.8 us
  blocking collectives  66.4 us (92%)
  Pallas kernels  3.65 us (5%)
    all_to_all x5, blocking collectives, exchange(): return lax.all_to_all(blocks, axis, 0, 0, axis_index_groups=groups)  66.4 us

profile of v8, /device:TPU:6, one launch (start us, length us, event | category | flops | bytes accessed | tf_op | source)
XLA Modules:
  0.0 70.8 jit_solution(466837197115998224)
XLA Ops:
  0.6 0.0 copy-start
  0.7 1.4 %shard_map.76 = (bf16[16,8,512]{2,1,0:T(8,128)(2,1)S(1)}, bf16[160,128]{1,0:T(8,128)(2,1)S(1)}) custom-call(s32[1]{0:T(128)} %bitcast.1.first_core_ref, bf16[320,512]{1,0:T(8,128)(2,1)} %bitcast.6, bf16[5120,128]{1,0:T(8,128)(2,1)} %p_ref.1), custom_call_target="tpu_custom_call" | custom-call | flops 41943040 | bytes 409600 | tf_op jit(solution)/shard_map/pallas_call | solution.py:86
  2.1 11.5 %all_to_all.30.parts_ref = bf16[16,8,512]{2,1,0:T(8,128)(2,1)S(1)} all-to-all(bf16[16,8,512]{2,1,0:T(8,128)(2,1)S(1)} %get-tuple-element.14), channel_id=1, replica_groups={{9,1,0,3,2,15,14,5,4,13,12,7,6,11,10,8},{25,17,16,19,18,31,30,21,20,29,..., dimensions={0} | all-to-all | bytes 262144 | tf_op jit(solution)/shard_map/all_to_all | solution.py:20
  13.6 11.2 %all_to_all.31.low_ref = bf16[16,8,512]{2,1,0:T(8,128)(2,1)S(1)} all-to-all(bf16[16,8,512]{2,1,0:T(8,128)(2,1)S(1)} %shard_map.77), channel_id=1, replica_groups={{9,1,0,3,2,15,14,5,4,13,12,7,6,11,10,8},{25,17,16,19,18,31,30,21,20,29,..., dimensions={0} | all-to-all | bytes 262144 | tf_op jit(solution)/shard_map/all_to_all | solution.py:20
  24.9 0.0 copy-done
  24.9 0.7 shard_map.78
  25.5 0.0 copy-start.1
  25.5 0.0 copy-start.2
  25.6 26.9 %conditional.1 = (f32[4,1600]{1,0:T(4,128)S(1)}) conditional(s32[]{:T(128)} %convert_element_type.10, bf16[32,4,1600]{2,1,0:T(4,128)(2,1)S(1)} %shard_map.78, bf16[32,4,1600]{2,1,0:T(4,128)(2,1)S(1)} %shard_map.78), branch_computations={%region_0.2_spmd, %region_2.4_spmd} | conditional | flops 403200 | bytes 1766408 | solution.py:248
  25.6 13.2 %all_to_all.28.parts_ref = bf16[4,8,4,1600]{3,2,1,0:T(4,128)(2,1)S(1)} all-to-all(bf16[4,8,4,1600]{3,2,1,0:T(4,128)(2,1)S(1)} %bitcast.4), channel_id=1, replica_groups={{256,0,128,384},{272,16,144,400},{288,32,160,416},{304,48,176,432},{320..., dimensions={0} | all-to-all | bytes 819200 | tf_op jit(solution)/shard_map/cond/branch_1_fun/all_to_all | solution.py:20
  38.8 0.2 branch_1_fun.1
  39.0 13.5 %all_to_all.29 = bf16[8,4,1600]{2,1,0:T(4,128)(2,1)S(1)} all-to-all(bf16[8,4,1600]{2,1,0:T(4,128)(2,1)S(1)} %branch_1_fun.1), channel_id=1, replica_groups={{64,0,16,112,32,96,48,80},{192,128,144,240,160,224,176,208},{320,256,27..., dimensions={0} | all-to-all | bytes 204800 | tf_op jit(solution)/shard_map/cond/branch_1_fun/all_to_all | solution.py:20
  52.4 0.1 convert_reduce_fusion.1
  52.5 0.0 copy-done.1
  52.5 0.0 copy-done.2
  52.5 0.2 shard_map.79
  52.7 17.0 %all_to_all.32.dirs_ref = bf16[32,4,1600]{2,1,0:T(4,128)(2,1)S(1)} all-to-all(bf16[32,4,1600]{2,1,0:T(4,128)(2,1)S(1)} %get-tuple-element.15), channel_id=1, replica_groups={{320,256,272,368,288,352,304,336,64,0,16,112,32,96,48,80,192,128,144,24..., dimensions={0} | all-to-all | bytes 819200 | tf_op jit(solution)/shard_map/all_to_all | solution.py:20
  69.7 1.2 %shard_map.80 = (bf16[2,160,800]{2,1,0:T(8,128)(2,1)}, f32[2,4,800]{2,1,0:T(4,128)}, f32[2,4,800]{2,1,0:T(4,128)}) custom-call(bf16[160,128]{1,0:T(8,128)(2,1)S(1)} %get-tuple-element.13.rows_ref, bf16[32,4,1600]{2,1,0:T(4,128)(2,1)S(1)} %all_to_all.32.dirs_ref, f32[2,4,800]{2,1,0:T(4,128)S(1)} %get-tuple-element.16.first_ref, ...), custom_call_target="tpu_custom_call" | custom-call | flops 65536000 | bytes 512000 | tf_op jit(solution)/shard_map/pallas_call | solution.py:226
  (1 shorter events, 0.0 us)
Async XLA Ops:
  0.6 24.2 %copy-start = (bf16[2,512,800]{1,2,0:T(8,128)(2,1)S(1)}, bf16[2,512,800]{1,2,0:T(8,128)(2,1)}, u32[]{:S(2)}) copy-start(bf16[2,512,800]{1,2,0:T(8,128)(2,1)} %param.8) | copy-start | bytes 4915204
  25.5 27.0 %copy-start.1 = (f32[2,4,800]{2,1,0:T(4,128)S(1)}, f32[2,4,800]{2,1,0:T(4,128)}, u32[]{:S(2)}) copy-start(f32[2,4,800]{2,1,0:T(4,128)} %first_ref.1) | copy-start | bytes 76804
  25.5 27.0 %copy-start.2 = (f32[2,4,800]{2,1,0:T(4,128)S(1)}, f32[2,4,800]{2,1,0:T(4,128)}, u32[]{:S(2)}) copy-start(f32[2,4,800]{2,1,0:T(4,128)} %second_ref.1) | copy-start | bytes 76804

commit v9 on v8

--- a/solution.py
+++ b/solution.py
@@ -9,7 +9,7 @@
 SECOND_FIX = 1.0 - 0.999**10
 PARAMS = pltpu.CompilerParams(vmem_limit_bytes=16 * 1024 * 1024)
 CHIPS_Z = 8
-LAST_X, LAST_Y, LAST_Z = 2, 4, 4
+LAST_X, LAST_Y, LAST_Z = 2, 4, 6
 CORES = 2
 SMEM = pl.BlockSpec(memory_space=pltpu.SMEM)
 VMEM = pl.BlockSpec(memory_space=pltpu.VMEM)

time: 72.3 us -> 71.9 us (level)
  the two profiles are of different devices: /device:TPU:6 before, /device:TPU:32 now
where the time goes in v9:
time: 71.9 us; the launch traced here: 71.5 us
  blocking collectives  67.1 us (93%)
  Pallas kernels  3.64 us (5%)
    all_to_all x5, blocking collectives, exchange(): return lax.all_to_all(blocks, axis, 0, 0, axis_index_groups=groups)  67.1 us

profile of v9, /device:TPU:32, one launch (start us, length us, event | category | flops | bytes accessed | tf_op | source)
XLA Modules:
  0.0 71.5 jit_solution(1929147398434350900)
XLA Ops:
  0.6 0.0 copy-start
  0.7 1.4 %shard_map.76 = (bf16[16,8,512]{2,1,0:T(8,128)(2,1)S(1)}, bf16[160,128]{1,0:T(8,128)(2,1)S(1)}) custom-call(s32[1]{0:T(128)} %bitcast.1.first_core_ref, bf16[320,512]{1,0:T(8,128)(2,1)} %bitcast.6, bf16[5120,128]{1,0:T(8,128)(2,1)} %p_ref.1), custom_call_target="tpu_custom_call" | custom-call | flops 41943040 | bytes 409600 | tf_op jit(solution)/shard_map/pallas_call | solution.py:86
  2.1 15.6 %all_to_all.30.parts_ref = bf16[16,8,512]{2,1,0:T(8,128)(2,1)S(1)} all-to-all(bf16[16,8,512]{2,1,0:T(8,128)(2,1)S(1)} %get-tuple-element.14), channel_id=1, replica_groups={{9,1,0,3,2,15,14,5,4,13,12,7,6,11,10,8},{25,17,16,19,18,31,30,21,20,29,..., dimensions={0} | all-to-all | bytes 262144 | tf_op jit(solution)/shard_map/all_to_all | solution.py:20
  17.8 11.3 %all_to_all.31.low_ref = bf16[16,8,512]{2,1,0:T(8,128)(2,1)S(1)} all-to-all(bf16[16,8,512]{2,1,0:T(8,128)(2,1)S(1)} %shard_map.77), channel_id=1, replica_groups={{9,1,0,3,2,15,14,5,4,13,12,7,6,11,10,8},{25,17,16,19,18,31,30,21,20,29,..., dimensions={0} | all-to-all | bytes 262144 | tf_op jit(solution)/shard_map/all_to_all | solution.py:20
  29.0 0.0 copy-done
  29.0 0.7 shard_map.78
  29.7 0.0 copy-start.1
  29.7 0.0 copy-start.2
  29.7 23.2 %conditional.1 = (f32[4,1600]{1,0:T(4,128)S(1)}) conditional(s32[]{:T(128)} %convert_element_type.10, bf16[32,4,1600]{2,1,0:T(4,128)(2,1)S(1)} %shard_map.78, bf16[32,4,1600]{2,1,0:T(4,128)(2,1)S(1)} %shard_map.78), branch_computations={%region_0.2_spmd, %region_2.4_spmd} | conditional | flops 403200 | bytes 1766408 | solution.py:248
  29.8 8.8 %all_to_all.28.parts_ref = bf16[4,8,4,1600]{3,2,1,0:T(4,128)(2,1)S(1)} all-to-all(bf16[4,8,4,1600]{3,2,1,0:T(4,128)(2,1)S(1)} %bitcast.4), channel_id=1, replica_groups={{256,0,128,384},{272,16,144,400},{288,32,160,416},{304,48,176,432},{320..., dimensions={0} | all-to-all | bytes 819200 | tf_op jit(solution)/shard_map/cond/branch_1_fun/all_to_all | solution.py:20
  38.6 0.2 branch_1_fun.1
  38.8 14.1 %all_to_all.29 = bf16[8,4,1600]{2,1,0:T(4,128)(2,1)S(1)} all-to-all(bf16[8,4,1600]{2,1,0:T(4,128)(2,1)S(1)} %branch_1_fun.1), channel_id=1, replica_groups={{96,32,48,16,64,0,80,112},{224,160,176,144,192,128,208,240},{352,288,30..., dimensions={0} | all-to-all | bytes 204800 | tf_op jit(solution)/shard_map/cond/branch_1_fun/all_to_all | solution.py:20
  52.8 0.1 convert_reduce_fusion.1
  52.9 0.0 copy-done.1
  52.9 0.0 copy-done.2
  52.9 0.2 shard_map.79
  53.1 17.3 %all_to_all.32.dirs_ref = bf16[32,4,1600]{2,1,0:T(4,128)(2,1)S(1)} all-to-all(bf16[32,4,1600]{2,1,0:T(4,128)(2,1)S(1)} %get-tuple-element.15), channel_id=1, replica_groups={{352,288,304,272,320,256,336,368,96,32,48,16,64,0,80,112,224,160,176,14..., dimensions={0} | all-to-all | bytes 819200 | tf_op jit(solution)/shard_map/all_to_all | solution.py:20
  70.4 1.2 %shard_map.80 = (bf16[2,160,800]{2,1,0:T(8,128)(2,1)}, f32[2,4,800]{2,1,0:T(4,128)}, f32[2,4,800]{2,1,0:T(4,128)}) custom-call(bf16[160,128]{1,0:T(8,128)(2,1)S(1)} %get-tuple-element.13.rows_ref, bf16[32,4,1600]{2,1,0:T(4,128)(2,1)S(1)} %all_to_all.32.dirs_ref, f32[2,4,800]{2,1,0:T(4,128)S(1)} %get-tuple-element.16.first_ref, ...), custom_call_target="tpu_custom_call" | custom-call | flops 65536000 | bytes 512000 | tf_op jit(solution)/shard_map/pallas_call | solution.py:226
  (1 shorter events, 0.0 us)
Async XLA Ops:
  0.6 28.4 %copy-start = (bf16[2,512,800]{1,2,0:T(8,128)(2,1)S(1)}, bf16[2,512,800]{1,2,0:T(8,128)(2,1)}, u32[]{:S(2)}) copy-start(bf16[2,512,800]{1,2,0:T(8,128)(2,1)} %param.8) | copy-start | bytes 4915204
  29.7 23.2 %copy-start.1 = (f32[2,4,800]{2,1,0:T(4,128)S(1)}, f32[2,4,800]{2,1,0:T(4,128)}, u32[]{:S(2)}) copy-start(f32[2,4,800]{2,1,0:T(4,128)} %first_ref.1) | copy-start | bytes 76804
  29.7 23.2 %copy-start.2 = (f32[2,4,800]{2,1,0:T(4,128)S(1)}, f32[2,4,800]{2,1,0:T(4,128)}, u32[]{:S(2)}) copy-start(f32[2,4,800]{2,1,0:T(4,128)} %second_ref.1) | copy-start | bytes 76804

commit v10 on v9

--- a/solution.py
+++ b/solution.py
@@ -10,6 +10,7 @@
 PARAMS = pltpu.CompilerParams(vmem_limit_bytes=16 * 1024 * 1024)
 CHIPS_Z = 8
 LAST_X, LAST_Y, LAST_Z = 2, 4, 6
+GATHER_Z = 4
 CORES = 2
 SMEM = pl.BlockSpec(memory_space=pltpu.SMEM)
 VMEM = pl.BlockSpec(memory_space=pltpu.VMEM)
@@ -25,9 +26,9 @@
     return [(last + step) % n for step in steps]
 
 
-def dp_order(n_dp):
+def dp_order(n_dp, last_z=LAST_Z):
     n_x = n_dp // CHIPS_Z
-    return [x * CHIPS_Z + z for x in far_first(n_x, LAST_X) for z in far_first(CHIPS_Z, LAST_Z)]
+    return [x * CHIPS_Z + z for x in far_first(n_x, LAST_X) for z in far_first(CHIPS_Z, last_z)]
 
 
 def tensor_order(n_tensor):
@@ -199,7 +200,7 @@
     rows_ref, dirs_ref, first_ref, second_ref, out_ref, new_first_ref, new_second_ref, buf, sems
 ):
     n_dp, columns = dirs_ref.shape[0], out_ref.shape[2]
-    order = dp_order(n_dp)
+    order = dp_order(n_dp, GATHER_Z)
     copies = [
         pltpu.make_async_copy(first_ref, new_first_ref, sems.at[2]),
         pltpu.make_async_copy(second_ref, new_second_ref, sems.at[3]),
@@ -247,7 +248,7 @@
     sent = project(low, out_grads.transpose(0, 2, 1), n_dp)
     own = lax.cond(first_core, scatter_by_axis, scatter_at_once, sent)
     direction, new_first, new_second = adam(own, first_moment, second_moment, n_dp)
-    every = exchange(direction, "dp", [dp_order(n_dp)])
+    every = exchange(direction, "dp", [dp_order(n_dp, GATHER_Z)])
     return expand(rows, every, new_first, new_second)
 
 

time: 71.9 us -> 71.8 us (level)
  the two profiles are of different devices: /device:TPU:32 before, /device:TPU:6 now
where the time goes in v10:
time: 71.8 us; the launch traced here: 71 us
  blocking collectives  66.5 us (93%)
  Pallas kernels  3.65 us (5%)
    all_to_all x5, blocking collectives, exchange(): return lax.all_to_all(blocks, axis, 0, 0, axis_index_groups=groups)  66.5 us

profile of v10, /device:TPU:6, one launch (start us, length us, event | category | flops | bytes accessed | tf_op | source)
XLA Modules:
  0.0 71.0 jit_solution(15214285129872349792)
XLA Ops:
  0.6 0.0 copy-start
  0.7 1.4 %shard_map.76 = (bf16[16,8,512]{2,1,0:T(8,128)(2,1)S(1)}, bf16[160,128]{1,0:T(8,128)(2,1)S(1)}) custom-call(s32[1]{0:T(128)} %bitcast.1.first_core_ref, bf16[320,512]{1,0:T(8,128)(2,1)} %bitcast.6, bf16[5120,128]{1,0:T(8,128)(2,1)} %p_ref.1), custom_call_target="tpu_custom_call" | custom-call | flops 41943040 | bytes 409600 | tf_op jit(solution)/shard_map/pallas_call | solution.py:87
  2.1 11.5 %all_to_all.30.parts_ref = bf16[16,8,512]{2,1,0:T(8,128)(2,1)S(1)} all-to-all(bf16[16,8,512]{2,1,0:T(8,128)(2,1)S(1)} %get-tuple-element.14), channel_id=1, replica_groups={{9,1,0,3,2,15,14,5,4,13,12,7,6,11,10,8},{25,17,16,19,18,31,30,21,20,29,..., dimensions={0} | all-to-all | bytes 262144 | tf_op jit(solution)/shard_map/all_to_all | solution.py:21
  13.6 11.2 %all_to_all.31.low_ref = bf16[16,8,512]{2,1,0:T(8,128)(2,1)S(1)} all-to-all(bf16[16,8,512]{2,1,0:T(8,128)(2,1)S(1)} %shard_map.77), channel_id=1, replica_groups={{9,1,0,3,2,15,14,5,4,13,12,7,6,11,10,8},{25,17,16,19,18,31,30,21,20,29,..., dimensions={0} | all-to-all | bytes 262144 | tf_op jit(solution)/shard_map/all_to_all | solution.py:21
  24.9 0.0 copy-done
  24.9 0.7 shard_map.78
  25.5 0.0 copy-start.1
  25.5 0.0 copy-start.2
  25.6 27.3 %conditional.1 = (f32[4,1600]{1,0:T(4,128)S(1)}) conditional(s32[]{:T(128)} %convert_element_type.10, bf16[32,4,1600]{2,1,0:T(4,128)(2,1)S(1)} %shard_map.78, bf16[32,4,1600]{2,1,0:T(4,128)(2,1)S(1)} %shard_map.78), branch_computations={%region_0.2_spmd, %region_2.4_spmd} | conditional | flops 403200 | bytes 1766408 | solution.py:249
  25.6 13.2 %all_to_all.28.parts_ref = bf16[4,8,4,1600]{3,2,1,0:T(4,128)(2,1)S(1)} all-to-all(bf16[4,8,4,1600]{3,2,1,0:T(4,128)(2,1)S(1)} %bitcast.4), channel_id=1, replica_groups={{256,0,128,384},{272,16,144,400},{288,32,160,416},{304,48,176,432},{320..., dimensions={0} | all-to-all | bytes 819200 | tf_op jit(solution)/shard_map/cond/branch_1_fun/all_to_all | solution.py:21
  38.8 0.2 branch_1_fun.1
  39.0 13.8 %all_to_all.29 = bf16[8,4,1600]{2,1,0:T(4,128)(2,1)S(1)} all-to-all(bf16[8,4,1600]{2,1,0:T(4,128)(2,1)S(1)} %branch_1_fun.1), channel_id=1, replica_groups={{96,32,48,16,64,0,80,112},{224,160,176,144,192,128,208,240},{352,288,30..., dimensions={0} | all-to-all | bytes 204800 | tf_op jit(solution)/shard_map/cond/branch_1_fun/all_to_all | solution.py:21
  52.7 0.1 convert_reduce_fusion.1
  52.8 0.0 copy-done.1
  52.8 0.0 copy-done.2
  52.8 0.2 shard_map.79
  53.0 16.8 %all_to_all.32.dirs_ref = bf16[32,4,1600]{2,1,0:T(4,128)(2,1)S(1)} all-to-all(bf16[32,4,1600]{2,1,0:T(4,128)(2,1)S(1)} %get-tuple-element.15), channel_id=1, replica_groups={{320,256,272,368,288,352,304,336,64,0,16,112,32,96,48,80,192,128,144,24..., dimensions={0} | all-to-all | bytes 819200 | tf_op jit(solution)/shard_map/all_to_all | solution.py:21
  69.8 1.2 %shard_map.80 = (bf16[2,160,800]{2,1,0:T(8,128)(2,1)}, f32[2,4,800]{2,1,0:T(4,128)}, f32[2,4,800]{2,1,0:T(4,128)}) custom-call(bf16[160,128]{1,0:T(8,128)(2,1)S(1)} %get-tuple-element.13.rows_ref, bf16[32,4,1600]{2,1,0:T(4,128)(2,1)S(1)} %all_to_all.32.dirs_ref, f32[2,4,800]{2,1,0:T(4,128)S(1)} %get-tuple-element.16.first_ref, ...), custom_call_target="tpu_custom_call" | custom-call | flops 65536000 | bytes 512000 | tf_op jit(solution)/shard_map/pallas_call | solution.py:227
  (1 shorter events, 0.0 us)
Async XLA Ops:
  0.6 24.2 %copy-start = (bf16[2,512,800]{1,2,0:T(8,128)(2,1)S(1)}, bf16[2,512,800]{1,2,0:T(8,128)(2,1)}, u32[]{:S(2)}) copy-start(bf16[2,512,800]{1,2,0:T(8,128)(2,1)} %param.8) | copy-start | bytes 4915204
  25.5 27.3 %copy-start.1 = (f32[2,4,800]{2,1,0:T(4,128)S(1)}, f32[2,4,800]{2,1,0:T(4,128)}, u32[]{:S(2)}) copy-start(f32[2,4,800]{2,1,0:T(4,128)} %first_ref.1) | copy-start | bytes 76804
  25.5 27.3 %copy-start.2 = (f32[2,4,800]{2,1,0:T(4,128)S(1)}, f32[2,4,800]{2,1,0:T(4,128)}, u32[]{:S(2)}) copy-start(f32[2,4,800]{2,1,0:T(4,128)} %second_ref.1) | copy-start | bytes 76804
